TPU v7x, 256 devices: a whole 4x4x8 slice. The times are simulated.
256 devices in a mesh: dp: 32 (over z, x), seq: 8 (over y, core).
Axes of the slice: x: 4, y: 4, z: 8, core: 2. Of those that a mesh axis runs over, the one named last changes fastest.
Arguments:
- patches: bfloat16 [32, 98304], P(None, ('dp', 'seq')), may hold values from -12 to 12
- segment_ids: int32 [32, 3072], P('dp'), may hold values from 0 to 15, never falling along the last dimension, each value on 1 to 2304 neighbouring positions
- regroup_plan: int32 [32, 5, 64], P('dp'), may hold values from 0 to 383, as said below
- input_weight: bfloat16 [32, 1280], replicated, may hold values from -1 to 1
- input_bias: float32 [1280], replicated, may hold values from -3 to 3
- skip_weight: bfloat16 [32, 1280], replicated, may hold values from -1 to 1
- hidden_weight: bfloat16 [1280, 1280], replicated, may hold values from -0.15625 to 0.15625
- output_bias: float32 [1280], replicated, may hold values from -3 to 3
- norm_gain: float32 [1280], replicated, may hold values from 0.1 to 1.9
- head_scale: float32 [8], replicated, may hold values from 1 to 4
- qkv_weight: bfloat16 [1280, 3, 640], replicated, may hold values from -0.15625 to 0.15625
- out_weight: bfloat16 [640, 1280], P(None, ('dp', 'seq')), may hold values from -0.25 to 0.25
- cotangent: bfloat16 [98304, 1280], P(('dp', 'seq')), may hold values from -0.3125 to 0.3125
Outputs:
- layer_out: bfloat16 [98304, 1280], P(('dp', 'seq'))
- out_grad: float32 [640, 1280], P(None, ('dp', 'seq'))
Inputs may be any that keep to these rules, and one draw needn't show every extreme that they name: `regroup_plan`: piece s * 8 + d of a window moves rows of source shard s to destination shard d: one piece for each pair, each moving one row or more. The pieces of a window cover each of the 384 rows of every source shard once and each of the 384 rows of every destination shard once. A piece moves at most 96 rows, and in every window some piece moves exactly 96. `segment_ids`: series ids never fall along a window's positions; one series of each window has exactly 2304 positions.
All inputs are finite; a program needn't handle non-finite values.
Results may differ from a plain program's by a relative error of at most 0.015.
Values may be sent and summed in bfloat16 or wider, within the bound.
A program may use at most 64 MiB of HBM per device.

v0:
```python
import math

import jax
import jax.numpy as jnp
from jax import lax
from jax.sharding import PartitionSpec as P

HD = 80


EPSILON = 1e-06
CONTRACT_FIRST = (((0,), (0,)), ((), ()))


def row_norm(values):
    return values * lax.rsqrt(jnp.mean(values * values, axis=-1, keepdims=True) + EPSILON)


def place_table(plan_rows, shard_rows, shard_count):
    source = plan_rows[0]
    first_row = plan_rows[1]
    row_count = plan_rows[2]
    target = plan_rows[3]
    offset_row = plan_rows[4]
    window_len = shard_rows * shard_count
    loader_row = jnp.arange(window_len, dtype=jnp.int32)
    begin_row = source * shard_rows + first_row
    inside = (loader_row[None, :] >= begin_row[:, None]) & (
        loader_row[None, :] < (begin_row + row_count)[:, None]
    )
    earlier = (
        (source[:, None] == source[None, :])
        & (target[:, None] == target[None, :])
        & (first_row[None, :] < first_row[:, None])
    )
    base_rank = jnp.sum(jnp.where(earlier, row_count[None, :], 0), axis=1)
    position = jnp.sum(
        jnp.where(
            inside, (target * shard_rows + offset_row - begin_row)[:, None] + loader_row[None, :], 0
        ),
        axis=0,
    )
    slot_rank = jnp.sum(
        jnp.where(inside, (base_rank - begin_row)[:, None] + loader_row[None, :], 0), axis=0
    )
    return (position, slot_rank)


def patch_block(columns, input_weight, input_bias, skip_weight, hidden_weight, output_bias):
    pre_act = (
        lax.dot_general(columns, input_weight, CONTRACT_FIRST, preferred_element_type=jnp.float32)
        + input_bias
    )
    hidden = jax.nn.silu(pre_act).astype(jnp.bfloat16)
    skipped = lax.dot_general(
        columns, skip_weight, CONTRACT_FIRST, preferred_element_type=jnp.float32
    )
    embedded = (
        jnp.dot(hidden, hidden_weight, preferred_element_type=jnp.float32) + skipped + output_bias
    )
    return embedded.astype(jnp.bfloat16)


def per_device(
    patches,
    segment_ids,
    regroup_plan,
    input_weight,
    input_bias,
    skip_weight,
    hidden_weight,
    output_bias,
    norm_gain,
    head_scale,
    qkv_weight,
    out_weight,
    cotangent,
):
    shard_count = lax.axis_size("seq")
    shard_index = lax.axis_index("seq")
    shard_rows = cotangent.shape[0]
    model_width = cotangent.shape[1]
    window_len = shard_rows * shard_count
    capacity = 2 * shard_rows // shard_count
    position, slot_rank = place_table(regroup_plan[0], shard_rows, shard_count)
    loader_row = jnp.arange(window_len, dtype=jnp.int32)
    own_rows = lax.dynamic_slice_in_dim(position, shard_index * shard_rows, shard_rows, 0)
    own_ranks = lax.dynamic_slice_in_dim(slot_rank, shard_index * shard_rows, shard_rows, 0)
    send_slot = own_rows // shard_rows * capacity + own_ranks
    send_table = (
        jnp.full((shard_count * capacity,), shard_rows, jnp.int32)
        .at[send_slot]
        .set(jnp.arange(shard_rows, dtype=jnp.int32))
    )
    landing = jnp.where(position // shard_rows == shard_index, position % shard_rows, shard_rows)
    receive_table = (
        jnp.zeros((shard_rows,), jnp.int32)
        .at[landing]
        .set(loader_row // shard_rows * capacity + slot_rank, mode="drop")
    )
    local_embed = patch_block(
        patches, input_weight, input_bias, skip_weight, hidden_weight, output_bias
    )
    padded = jnp.concatenate([local_embed, jnp.zeros((1, model_width), jnp.bfloat16)], axis=0)
    arrived = lax.all_to_all(padded[send_table], "seq", split_axis=0, concat_axis=0, tiled=True)
    embedded = arrived[receive_table]
    normed = (row_norm(embedded.astype(jnp.float32)) * norm_gain).astype(jnp.bfloat16)
    projected = jnp.dot(
        normed, qkv_weight.reshape(model_width, -1), preferred_element_type=jnp.float32
    )
    projected = projected.astype(jnp.bfloat16).reshape(shard_rows, 3, -1)
    head_rows = lax.all_to_all(projected, "seq", split_axis=2, concat_axis=0, tiled=True)
    local_width = head_rows.shape[2]
    local_heads = local_width // HD
    queries = row_norm(
        head_rows[:, 0].reshape(window_len, local_heads, HD).astype(jnp.float32)
    ).astype(jnp.bfloat16)
    key_rows = row_norm(
        head_rows[:, 1].reshape(window_len, local_heads, HD).astype(jnp.float32)
    ).astype(jnp.bfloat16)
    value_rows = head_rows[:, 2].reshape(window_len, local_heads, HD)
    factor = lax.dynamic_slice_in_dim(head_scale, shard_index * local_heads, local_heads, 0) * (
        1.0 / math.sqrt(HD)
    )
    segment_row = segment_ids[0]
    block_len = min(512, window_len)
    block_count = window_len // block_len
    pieces = []
    for block_index in range(block_count):
        query_first = block_index * block_len
        query_part = queries[query_first : query_first + block_len]
        query_pos = query_first + jnp.arange(block_len, dtype=jnp.int32)
        query_seg = segment_row[query_first : query_first + block_len]
        key_len = query_first + block_len
        key_part = lax.slice_in_dim(key_rows, 0, key_len, axis=0)
        value_part = lax.slice_in_dim(value_rows, 0, key_len, axis=0)
        key_seg = lax.slice_in_dim(segment_row, 0, key_len, axis=0)
        key_pos = jnp.arange(key_len, dtype=jnp.int32)
        scores = (
            jnp.einsum("qhd,khd->hqk", query_part, key_part, preferred_element_type=jnp.float32)
            * factor[:, None, None]
        )
        allowed = (query_seg[:, None] == key_seg[None, :]) & (
            key_pos[None, :] <= query_pos[:, None]
        )
        weights = jnp.where(allowed[None], jnp.exp(scores), 0.0)
        summed = jnp.einsum(
            "hqk,khd->qhd",
            weights.astype(jnp.bfloat16),
            value_part,
            preferred_element_type=jnp.float32,
        )
        summed, denominator = (summed, jnp.sum(weights, axis=-1))
        pieces.append(
            (summed / jnp.transpose(denominator)[:, :, None]).reshape(block_len, local_width)
        )
    attended = jnp.concatenate(pieces, axis=0).astype(jnp.bfloat16)
    returned = lax.all_to_all(attended, "seq", split_axis=0, concat_axis=1, tiled=True)
    branch = jnp.dot(
        returned,
        lax.all_gather(out_weight, ("dp", "seq"), axis=1, tiled=True),
        preferred_element_type=jnp.float32,
    )
    layer_out = (embedded.astype(jnp.float32) + branch).astype(jnp.bfloat16)
    grad_term = lax.dot_general(
        returned, cotangent, CONTRACT_FIRST, preferred_element_type=jnp.float32
    )
    out_grad = lax.psum_scatter(grad_term, ("dp", "seq"), scatter_dimension=1, tiled=True)
    return (layer_out, out_grad)


def solution(mesh):
    placed = (
        P(None, ("dp", "seq")),
        P("dp", None),
        P("dp", None, None),
        P(),
        P(),
        P(),
        P(),
        P(),
        P(),
        P(),
        P(),
        P(None, ("dp", "seq")),
        P(("dp", "seq"), None),
    )
    return jax.shard_map(
        per_device,
        mesh=mesh,
        in_specs=placed,
        out_specs=(P(("dp", "seq"), None), P(None, ("dp", "seq"))),
        check_vma=False,
    )
```

profile of v0, /device:TPU:1, one launch (start us, length us, event | category | flops | bytes accessed | tf_op | source)
XLA Modules:
  0.0 471.7 jit_solution(12129723158445891963)
XLA Ops:
  10.1 2.9 scatter_custom_fusion
  13.1 4.2 fusion.23
  17.3 2.0 fusion.9
  20.3 6.5 %gather_fusion = bf16[768,1280]{1,0:T(8,128)(2,1)} fusion(bf16[385,1280]{1,0:T(8,128)(2,1)} %concatenate.7, s32[1024]{0:T(1024)S(1)} %pad_clamp_fusion.1), kind=kCustom, calls=%fused_computation | custom fusion | bytes 3935232 | tf_op jit(solution)/shard_map/gather | solution.py:105
  26.9 7.5 %all-to-all-start = ((bf16[8,96,1280]{2,1,0:T(8,128)(2,1)}), bf16[8,96,1280]{2,1,0:T(8,128)(2,1)}, u32[]{:S(2)}, u32[]{:S(2)}) async-start(bf16[8,96,1280]{2,1,0:T(8,128)(2,1)} %bitcast.252), calls=%async_computation | async-start | bytes 3932160 | tf_op jit(solution)/shard_map/all_to_all | solution.py:105
  34.3 8.2 %copy.25 = bf16[1280,3,640]{0,2,1:T(8,128)(2,1)} copy(bf16[1280,3,640]{2,0,1:T(8,128)(2,1)} %param.23) | data formatting | bytes 9830400 | tf_op args[10]
  42.6 11.9 %scatter_custom_fusion.1 = s32[384]{0:T(512)S(1)} fusion(s32[3072]{0:T(1024)S(1)} %bitcast.265, s32[3072]{0:T(1024)S(1)} %get-tuple-element.36, s32[]{:T(128)} %constant.25.clone.1), kind=kCustom, calls=%fused_computation.154 | custom fusion | bytes 1540 | tf_op jit(solution)/shard_map/scatter | solution.py:99
  54.6 4.8 %all-to-all-done = bf16[8,96,1280]{2,1,0:T(8,128)(2,1)} async-done(((bf16[8,96,1280]{2,1,0:T(8,128)(2,1)}), bf16[8,96,1280]{2,1,0:T(8,128)(2,1)}, u32[]{:S(2)}, u32[]{:S(2)}) %all-to-all-start) | async-done | bytes 1966112 | tf_op jit(solution)/shard_map/all_to_all | solution.py:105
  59.4 5.6 %gather_fusion.1 = bf16[384,1280]{1,0:T(8,128)(2,1)} fusion(bf16[768,1280]{1,0:T(8,128)(2,1)} %bitcast.6, s32[1024]{0:T(1024)S(1)} %pad_clamp_fusion), kind=kCustom, calls=%fused_computation.1 | custom fusion | bytes 1967616 | tf_op jit(solution)/shard_map/gather | solution.py:106
  66.5 6.2 %convolution_convert_fusion = bf16[384,1920]{1,0:T(8,128)(2,1)} fusion(bf16[1280,1920]{0,1:T(8,128)(2,1)} %bitcast.255, bf16[384,1280]{1,0:T(8,128)(2,1)} %gather_fusion.1, f32[1280]{0:T(1024)S(1)} %copy-done.7, f32[384]{0:T(512)S(1)} %add_rsqrt_fusion.2), kind=kOutput, calls=%fused_computation.27 | convolution fusion | flops 1890140160 | bytes 7379456 | tf_op jit(solution)/shard_map/dot_general | solution.py:108
  72.6 2.6 copy.26
  75.2 3.9 copy.27
  79.1 5.2 %all-to-all-start.1 = ((bf16[384,3,640]{0,1,2:T(4,128)(2,1)}), bf16[384,3,640]{0,1,2:T(4,128)(2,1)}, u32[]{:S(2)}, u32[]{:S(2)}) async-start(bf16[384,3,640]{0,1,2:T(4,128)(2,1)} %copy.27), calls=%async_computation.1 | async-start | bytes 3932160 | tf_op jit(solution)/shard_map/all_to_all | solution.py:112
  86.7 22.7 %all-to-all-done.1 = bf16[384,3,640]{0,1,2:T(4,128)(2,1)} async-done(((bf16[384,3,640]{0,1,2:T(4,128)(2,1)}), bf16[384,3,640]{0,1,2:T(4,128)(2,1)}, u32[]{:S(2)}, u32[]{:S(2)}) %all-to-all-start.1) | async-done | bytes 1474592 | tf_op jit(solution)/shard_map/all_to_all | solution.py:112
  109.4 1.7 copy.28
  115.9 1.9 fusion.124
  118.7 2.3 fusion.125
  121.9 2.7 fusion.126
  125.8 12.3 %all_to_all.46 = bf16[8,384,80]{1,2,0:T(8,128)(2,1)S(1)} all-to-all(bf16[8,384,80]{1,2,0:T(8,128)(2,1)S(1)} %bitcast.258), channel_id=1, replica_groups=mesh['dp'=32,'seq'=8] {'seq'}, dimensions={0} | all-to-all | bytes 983040 | tf_op jit(solution)/shard_map/all_to_all | solution.py:158
  138.9 2.9 fusion.127
  141.8 53.6 %all-gather.3.cloned.1.call-done = bf16[256,5,640]{2,1,0:T(8,128)(2,1)} async-done(((bf16[1,5,640]{2,1,0:T(8,128)(2,1)}), bf16[256,5,640]{2,1,0:T(8,128)(2,1)}) %all-gather.3.cloned.1.call-update) | async-done | bytes 1638416 | tf_op jit(solution)/shard_map/all_gather | solution.py:161
  195.4 4.1 reshape.456
  199.5 3.8 fusion.10
  203.3 260.2 %all-reduce.4.cloned.1.call-done = f32[640,1280]{0,1:T(8,128)} async-done(((f32[640,1280]{0,1:T(8,128)}), f32[640,1280]{0,1:T(8,128)}) %all-reduce.4.cloned.1.call-update) | async-done | bytes 3276816
  (68 shorter events, 16.9 us)
Async XLA Ops:
  7.2 5.9 %copy-start = (bf16[1280,1280]{1,0:T(8,128)(2,1)S(1)}, bf16[1280,1280]{1,0:T(8,128)(2,1)}, u32[]{:S(2)}) copy-start(bf16[1280,1280]{1,0:T(8,128)(2,1)} %param.19) | copy-start | bytes 9830404
  13.1 4.2 copy-start.4
  13.1 4.2 copy-start.5
  13.1 4.2 copy-start.6
  26.9 32.5 %all-to-all-start = ((bf16[8,96,1280]{2,1,0:T(8,128)(2,1)}), bf16[8,96,1280]{2,1,0:T(8,128)(2,1)}, u32[]{:S(2)}, u32[]{:S(2)}) async-start(bf16[8,96,1280]{2,1,0:T(8,128)(2,1)} %bitcast.252), calls=%async_computation | async-start | bytes 3932160 | tf_op jit(solution)/shard_map/all_to_all | solution.py:105
  59.4 7.1 %copy-start.7 = (f32[1280]{0:T(1024)S(1)}, f32[1280]{0:T(1024)}, u32[]{:S(2)}) copy-start(f32[1280]{0:T(1024)} %param.21) | copy-start | bytes 15364
  79.1 6.2 %copy-start.8 = (f32[8]{0:T(128)S(1)}, f32[8]{0:T(128)}, u32[]{:S(2)}) copy-start(f32[8]{0:T(128)} %param.22) | copy-start | bytes 100
  79.1 7.5 %copy-start.3 = (s32[1,3072]{1,0:T(1,128)S(1)}, s32[1,3072]{1,0:T(1,128)}, u32[]{:S(2)}) copy-start(s32[1,3072]{1,0:T(1,128)} %param.14) | copy-start | bytes 36868
  79.1 30.3 %all-to-all-start.1 = ((bf16[384,3,640]{0,1,2:T(4,128)(2,1)}), bf16[384,3,640]{0,1,2:T(4,128)(2,1)}, u32[]{:S(2)}, u32[]{:S(2)}) async-start(bf16[384,3,640]{0,1,2:T(4,128)(2,1)} %copy.27), calls=%async_computation.1 | async-start | bytes 3932160 | tf_op jit(solution)/shard_map/all_to_all | solution.py:112
  84.3 111.1 %all-gather.3.cloned.1.call-start = ((), (), s32[]{:S(2)}) async-start(), calls=%async_computation.3 | async-start | bytes 2631680 | tf_op jit(solution)/shard_map/all_gather | solution.py:161
  85.0 378.5 %all-reduce.4.cloned.1.call-start = ((), (), s32[]{:S(2)}) async-start(), calls=%async_computation.4 | async-start | bytes 6553600
  111.9 0.7 slice-start
  114.9 1.1 slice-start.1
  124.6 14.3 %copy-start.2 = (bf16[384,1280]{1,0:T(8,128)(2,1)S(1)}, bf16[384,1280]{1,0:T(8,128)(2,1)}, u32[]{:S(2)}) copy-start(bf16[384,1280]{1,0:T(8,128)(2,1)} %param.25) | copy-start | bytes 2949124
  138.1 0.8 copy-start.1
Sparse Core Ops, SparseCore 0:
  88.9 106.5 all-gather.2
  200.9 262.5 all-reduce.3
where the time goes:
time: 474 us; the launch traced here: 472 us
  waiting for transfers between devices  342 us (72%)
  local copies, waits for them, and re-layouts  52.6 us (11%)
  matrix products  32.7 us (7%)
  between operations  15 us (3%)
  starting transfers between devices  12.9 us (3%)
  blocking collectives  12.3 us (3%)
    unnamed x3, waiting for transfers between devices  261 us
    all_gather x1, waiting for transfers between devices, per_device(): lax.all_gather(out_weight, ('dp', 'seq'), axis=1, tiled=True)  53.6 us
    all_to_all x1, waiting for transfers between devices, per_device(): lax.all_to_all(projected, 'seq', split_axis=2, concat_axis=0, tiled=True)  22.7 us
    unnamed x21, local copies, waits for them, and re-layouts  14.5 us
    all_to_all x1, blocking collectives, per_device(): lax.all_to_all(attended, 'seq', split_axis=0, concat_axis=1, tiled=True)  12.3 us
    scatter x1, local copies, waits for them, and re-layouts, per_device(): receive_table = jnp.zeros((shard_rows,), jnp.int32).at[landing].set(loade...  11.9 us
    dot_general x6, matrix products, per_device(): jnp.einsum('qhd,khd->hqk', query_part, key_part, preferred_element_type=j...  9.7 us
  transfers between devices with their start and end apart: 4, of which 4 were waited for; matrix products, arithmetic and copies ran while one was open for 10% of the time, Pallas kernels for 0%

commit v1 on v0

v1 whole, which is shorter than its diff:
```python
import functools
import math

import jax
import jax.numpy as jnp
from jax import lax
from jax.experimental import pallas as pl
from jax.experimental.pallas import tpu as pltpu
from jax.sharding import PartitionSpec as P

HD = 80
LANES = 128
ZN, XN, YN = 8, 4, 4
SEQ = 8
ROWS = 384
WIN = ROWS * SEQ
D = 1280
HW = 640
PATCH = 32
COLS = 5
GROUP = COLS * SEQ
EPS = 1e-06
MASKED = 2048.0
LOG2E = 1.4426950408889634
MESH = pl.DeviceIdType.MESH
BF = jnp.bfloat16
F32 = jnp.float32
NT = (((1,), (1,)), ((), ()))


def iota(shape, dim):
    return lax.broadcasted_iota(jnp.int32, shape, dim)


def dot(a, b):
    return jnp.dot(a, b, preferred_element_type=F32)


def dot_nt(a, b):
    return lax.dot_general(a, b, NT, preferred_element_type=F32)


def whole_layer(
    x_ref,
    seg_ref,
    plan_ref,
    win_ref,
    bin_ref,
    wskip_ref,
    wh_hbm,
    ob_ref,
    gain_ref,
    hs_ref,
    qkvw_hbm,
    ow_ref,
    cot_hbm,
    lo_ref,
    og_ref,
    wh,
    qkvw,
    cot,
    cot_t,
    xg,
    win8,
    wskip8,
    wsel,
    qkv,
    msend,
    emb_own,
    ow_send,
    w_land,
    wx,
    wt,
    att_send,
    ret,
    p_own,
    p_send,
    p_land,
    ya,
    ya_land,
    xb,
    xb_land,
    ax,
    ax_land,
    by,
    by_land,
    block40,
    fs,
    fs_land,
    ld_sem,
    x_s,
    x_r,
    w1_s,
    w1_r,
    w2_s,
    w2_r,
    w3_s,
    w3_r,
    w4_s,
    w4_r,
    m_s,
    m_r,
    a_s,
    a_r,
    p_s,
    p_r,
    ya_s,
    ya_r,
    xb_s,
    xb_r,
    ax_s,
    ax_r,
    by_s,
    by_r,
    f_s,
    f_r,
):
    dp = lax.axis_index("dp")
    s = lax.axis_index("seq")
    z = dp // XN
    xx = dp % XN
    y = s // 2
    c = s % 2
    mate = y * 2 + (1 - c)
    zmine = c * YN + y
    ownseq = (z % YN) * 2 + z // YN
    on_own = z == zmine

    def rcopy(src, dst, ssem, rsem, dp_t, seq_t):
        return pltpu.make_async_remote_copy(
            src_ref=src,
            dst_ref=dst,
            send_sem=ssem,
            recv_sem=rsem,
            device_id=(dp_t, seq_t),
            device_id_type=MESH,
        )

    def dpi(zz, x2):
        return zz * XN + x2

    loads = [
        pltpu.make_async_copy(qkvw_hbm, qkvw, ld_sem.at[0]),
        pltpu.make_async_copy(wh_hbm, wh, ld_sem.at[1]),
        pltpu.make_async_copy(cot_hbm, cot, ld_sem.at[2]),
    ]
    for ld in loads:
        ld.start()

    bar = pltpu.get_barrier_semaphore()

    def greet(dp_t, seq_t):
        pl.semaphore_signal(bar, inc=1, device_id=(dp_t, seq_t), device_id_type=MESH)

    for k in range(1, SEQ):
        greet(dp, (s + k) % SEQ)
    for k in range(1, XN):
        greet(dpi(z, (xx + k) % XN), s)
    for k in range(1, ZN):
        greet(dpi((z + k) % ZN, xx), ownseq)

    @pl.when(jnp.logical_not(on_own))
    def _():
        greet(dp, ownseq)

    for t in range(SEQ):

        @pl.when(jnp.logical_not(on_own & (s == t)))
        def _():
            greet(dpi(zmine, xx), jnp.int32(t))

    ow_send[...] = jnp.zeros((8, HW), F32)
    ow_send[0:COLS, :] = ow_ref[...].astype(F32)
    for k in range(SEQ):
        win8[k * PATCH : (k + 1) * PATCH, :] = win_ref[...]
        wskip8[k * PATCH : (k + 1) * PATCH, :] = wskip_ref[...]
    xg[pl.ds(pl.multiple_of(s * PATCH, PATCH), PATCH), :] = x_ref[...]

    pl.semaphore_wait(bar, 7 + 3 + 16 - 2 * on_own.astype(jnp.int32))

    def x_copy(k, source):
        rows = xg.at[pl.ds(pl.multiple_of(source * PATCH, PATCH), PATCH), :]
        return rcopy(x_ref, rows, x_s.at[k], x_r.at[k], dp, (s + k) % SEQ)

    for k in range(1, SEQ):
        x_copy(k, s).start()

    def w1_copy(k):
        return rcopy(
            ow_send, w_land.at[s], w1_s.at[k], w1_r.at[s], dpi((z + k) % ZN, xx), ownseq
        )

    for k in range(1, ZN):
        w1_copy(k).start()

    @pl.when(jnp.logical_not(on_own))
    def _():
        w1_copy(0).start()

    @pl.when(on_own)
    def _():
        w_land[s] = ow_send[...]

    loads[0].wait()
    feature = iota((HW, 2 * LANES), 0)
    lane2 = iota((HW, 2 * LANES), 1)
    inner = lane2 % LANES
    head = jnp.where(lane2 < LANES, s, mate)
    pick = jnp.where((inner < HD) & (feature == head * HD + inner), 1.0, 0.0).astype(BF)
    for i in range(3):

        def pick_rows(r, carry, i=i):
            rows = pl.ds(pl.multiple_of(r * 256, 256), 256)
            part = dot(qkvw[i, rows, :], pick).astype(BF)
            wsel[rows, i * LANES : (i + 1) * LANES] = part[:, :LANES]
            wsel[rows, (3 + i) * LANES : (4 + i) * LANES] = part[:, LANES:]
            return carry

        lax.fori_loop(0, D // 256, pick_rows, 0)

    loads[2].wait()
    for i in range(2):
        cot_t[i] = jnp.transpose(cot[:, i * HW : (i + 1) * HW])
    loads[1].wait()
    for k in range(1, SEQ):
        x_copy(k, (s - k + SEQ) % SEQ).wait_recv()

    def w2_copy(k, source):
        return rcopy(
            wx.at[xx] if source is None else wx.at[xx],
            wx.at[xx if source is None else source],
            w2_s.at[k],
            w2_r.at[k],
            dpi(z, (xx + k) % XN),
            s,
        )

    def wt_rows(zz):
        return wt.at[pl.ds(pl.multiple_of(zz * 160, 32), 160), :]

    def zof(seq):
        return (seq % 2) * YN + seq // 2

    def w3_copy(k, source):
        block = zof(s) if source is None else zof(source)
        return rcopy(
            wt_rows(zof(s)), wt_rows(block), w3_s.at[k], w3_r.at[k], dp, ((y + k) % YN) * 2 + c
        )

    def w4_copy(k, core):
        block = wt_rows(core * YN + (y - k + YN) % YN)
        return rcopy(block, block, w4_s.at[k], w4_r.at[k], dp, mate)

    def m_copy(i, core):
        rows = pl.multiple_of((2 * i + core) * ROWS, ROWS)
        return rcopy(msend.at[i], qkv.at[pl.ds(rows, ROWS), :], m_s.at[i], m_r.at[i], dp, mate)

    lane = iota((ROWS, LANES), 1)
    seg_lane = (lane >= HD) & (lane < HD + 16)

    def embed_chunk(i, carry):
        chunk = 2 * i + c
        first_row = pl.multiple_of(chunk * ROWS, ROWS)
        pos = first_row + iota((ROWS, 64), 0)
        source, first, count = plan_ref[0], plan_ref[1], plan_ref[2]
        start = plan_ref[3] * ROWS + plan_ref[4]
        inside = (pos >= start) & (pos < start + count)
        code = jnp.where(inside, (source * 512 + first - start) + pos, 0)
        code = jnp.sum(code.astype(F32), axis=1, keepdims=True).astype(jnp.int32)
        row_of = code % 512
        shard_of = code // 512
        onehot = jnp.where(iota((ROWS, ROWS), 1) == row_of, 1.0, 0.0).astype(BF)
        spread = dot_nt(onehot, xg[...])
        cols = jnp.where(
            iota((ROWS, SEQ * PATCH), 1) // PATCH == shard_of, spread, 0.0
        ).astype(BF)
        half = (dot(cols, win8[...]) + bin_ref[...]) * 0.5
        hidden = (half + half * jnp.tanh(half)).astype(BF)
        emb = (dot(hidden, wh[...]) + dot(cols, wskip8[...]) + ob_ref[...]).astype(BF)

        @pl.when(i == y)
        def _():
            emb_own[...] = emb

        wide = emb.astype(F32)
        scale = lax.rsqrt(jnp.mean(wide * wide, axis=-1, keepdims=True) + EPS)
        normed = (wide * scale * gain_ref[...]).astype(BF)
        proj = dot(normed, wsel[...]).astype(BF)

        seg_row = seg_ref[:, pl.ds(first_row, ROWS)]
        marks = jnp.where(iota((LANES, ROWS), 0) - HD == seg_row, 1.0, 0.0)
        marks = jnp.transpose(marks)
        away = jnp.where(seg_lane, (marks - 1.0) * MASKED, 0.0)
        ones = jnp.where(lane == HD, 1.0, 0.0)
        parts = []
        for h in range(2):
            q = proj[:, (3 * h) * LANES : (3 * h + 1) * LANES].astype(F32)
            k = proj[:, (3 * h + 1) * LANES : (3 * h + 2) * LANES].astype(F32)
            v = proj[:, (3 * h + 2) * LANES : (3 * h + 3) * LANES].astype(F32)
            q = q * lax.rsqrt(jnp.sum(q * q, axis=-1, keepdims=True) * (1.0 / HD) + EPS)
            k = k * lax.rsqrt(jnp.sum(k * k, axis=-1, keepdims=True) * (1.0 / HD) + EPS)
            parts.append([(q + away).astype(BF), (k + marks).astype(BF), (v + ones).astype(BF)])
        for j in range(3):
            msend[i, :, j * LANES : (j + 1) * LANES] = parts[1][j]
        m_copy(i, c).start()
        for j in range(3):
            qkv[pl.ds(first_row, ROWS), j * LANES : (j + 1) * LANES] = parts[0][j]

        @pl.when(i == 0)
        def _():
            for t in range(SEQ):

                @pl.when(jnp.logical_not(on_own & (s == t)))
                def _():
                    rcopy(ow_send, w_land.at[t], w1_s.at[0], w1_r.at[t], dp, mate).wait_recv()

            block = jnp.concatenate([w_land[t, 0:COLS, :] for t in range(SEQ)], axis=0)
            block = jnp.concatenate([block, jnp.zeros((8, HW), F32)], axis=0)
            wx[xx] = block.astype(BF)
            for k in range(1, XN):
                w2_copy(k, None).start()

        @pl.when(i == 1)
        def _():
            for k in range(1, XN):
                w2_copy(k, (xx - k + XN) % XN).wait_recv()
            block = jnp.concatenate([wx[j, 0:GROUP, :].astype(F32) for j in range(XN)], axis=0)
            wt[pl.ds(pl.multiple_of(zmine * 160, 32), 160), :] = block.astype(BF)
            for k in range(1, YN):
                w3_copy(k, None).start()
            w4_copy(0, c).start()

        return carry

    lax.fori_loop(0, 4, embed_chunk, 0)

    for k in range(1, YN):
        w3_copy(k, ((y - k + YN) % YN) * 2 + c).wait_recv()
        w4_copy(k, c).start()
    for i in range(4):
        m_copy(i, 1 - c).wait_recv()

    factor = hs_ref[s] * (LOG2E / math.sqrt(HD))
    causal = iota((ROWS, ROWS), 0) >= iota((ROWS, ROWS), 1)

    def a_copy(block, source, k):
        rows = ret.at[pl.ds(pl.multiple_of(source * HD, 16), HD), :]
        return rcopy(att_send.at[block], rows, a_s.at[k], a_r.at[k], dp, (s + k) % SEQ)

    for b in reversed(range(SEQ)):
        q = qkv[b * ROWS : (b + 1) * ROWS, 0:LANES]
        total = jnp.zeros((ROWS, LANES), F32)
        edges = list(range(0, b * ROWS, 2 * ROWS)) + [b * ROWS]
        for lo, hi in zip(edges[:-1], edges[1:]):
            scores = dot_nt(q, qkv[lo:hi, LANES : 2 * LANES]) * factor
            total = total + dot(jnp.exp2(scores).astype(BF), qkv[lo:hi, 2 * LANES : 3 * LANES])
        lo, hi = b * ROWS, (b + 1) * ROWS
        scores = dot_nt(q, qkv[lo:hi, LANES : 2 * LANES]) * factor
        weights = jnp.where(causal, jnp.exp2(scores), 0.0).astype(BF)
        total = total + dot(weights, qkv[lo:hi, 2 * LANES : 3 * LANES])
        across = jnp.transpose(total)
        out = (across[0:HD, :] / across[HD : HD + 1, :]).astype(BF)
        att_send[b] = out

        @pl.when(s == b)
        def _():
            ret[pl.ds(pl.multiple_of(s * HD, 16), HD), :] = out

        @pl.when(s != b)
        def _():
            a_copy(b, s, (b - s + SEQ) % SEQ).start()

    for k in range(1, SEQ):
        a_copy(0, (s - k + SEQ) % SEQ, k).wait_recv()

    attended = ret[...]
    p_send[...] = dot_nt(cot_t[1 - c], attended)
    pair = rcopy(p_send, p_land, p_s.at[0], p_r.at[0], dp, mate)
    pair.start()
    p_own[...] = dot_nt(cot_t[c], attended)

    pair.wait_recv()
    summed = p_own[...] + p_land[...]
    p_own[...] = summed
    half_rows = summed.reshape(YN, XN, GROUP, HW)
    for j in range(YN):
        ya[j] = summed[j * 160 : (j + 1) * 160, 0:ROWS].astype(BF)
    pad = jnp.zeros((YN, 8, HW - ROWS), F32)
    for j in range(XN):
        xb[j] = jnp.concatenate([half_rows[:, j, :, ROWS:], pad], axis=1).astype(BF)

    def ya_copy(k):
        to = (y + k) % YN
        return rcopy(ya.at[to], ya_land.at[k], ya_s.at[k], ya_r.at[k], dp, to * 2 + c)

    def xb_copy(k):
        to = (xx + k) % XN
        return rcopy(xb.at[to], xb_land.at[k], xb_s.at[k], xb_r.at[k], dpi(z, to), s)

    for k in range(1, YN):
        ya_copy(k).start()
        xb_copy(k).start()

    for k in range(YN):
        w4_copy(k, 1 - c).wait_recv()
    rows = jnp.transpose(attended)
    for j in range(5):
        cols = slice(j * 256, (j + 1) * 256)
        branch = dot_nt(rows, wt[cols, :])
        lo_ref[:, cols] = (emb_own[:, cols].astype(F32) + branch).astype(BF)

    for k in range(1, YN):
        ya_copy(k).wait_recv()
    own = p_own[pl.ds(pl.multiple_of(y * 160, 32), 160), :]
    a_sum = own[:, 0:ROWS]
    for k in range(1, YN):
        a_sum = a_sum + ya_land[k].astype(F32)
    pad = jnp.zeros((8, ROWS), F32)
    block40[...] = jnp.zeros_like(block40)
    for j in range(XN):
        piece = a_sum[j * GROUP : (j + 1) * GROUP, :]
        ax[j] = jnp.concatenate([piece, pad], axis=0).astype(BF)

        @pl.when(xx == j)
        def _():
            block40[:, 0:ROWS] = piece

    def ax_copy(k):
        to = (xx + k) % XN
        return rcopy(ax.at[to], ax_land.at[k], ax_s.at[k], ax_r.at[k], dpi(z, to), s)

    for k in range(1, XN):
        ax_copy(k).start()

    for k in range(1, XN):
        xb_copy(k).wait_recv()
    pad = jnp.zeros((8, HW - ROWS), F32)
    for j in range(YN):
        begin = pl.multiple_of((j * XN + xx) * GROUP, 8)
        piece = p_own[pl.ds(begin, GROUP), ROWS:HW]
        for k in range(1, XN):
            piece = piece + xb_land[k, j].astype(F32)[0:GROUP, :]
        by[j] = jnp.concatenate([piece, pad], axis=0).astype(BF)

        @pl.when(y == j)
        def _():
            block40[:, ROWS:HW] = piece

    def by_copy(k):
        to = (y + k) % YN
        return rcopy(by.at[to], by_land.at[k], by_s.at[k], by_r.at[k], dp, to * 2 + c)

    for k in range(1, YN):
        by_copy(k).start()
    for k in range(1, XN):
        ax_copy(k).wait_recv()
    for k in range(1, YN):
        by_copy(k).wait_recv()
    left = block40[:, 0:ROWS]
    right = block40[:, ROWS:HW]
    for k in range(1, XN):
        left = left + ax_land[k].astype(F32)[0:GROUP, :]
        right = right + by_land[k].astype(F32)[0:GROUP, :]
    block40[:, 0:ROWS] = left
    block40[:, ROWS:HW] = right
    fs[...] = jnp.zeros_like(fs)
    for t in range(SEQ):
        fs[t, 0:COLS, :] = block40[t * COLS : (t + 1) * COLS, :]

    def f_copy(t):
        return rcopy(fs.at[t], fs_land.at[z], f_s.at[t], f_r.at[z], dpi(zmine, xx), jnp.int32(t))

    for t in range(SEQ):

        @pl.when(jnp.logical_not(on_own & (s == t)))
        def _():
            f_copy(t).start()

        @pl.when(on_own & (s == t))
        def _():
            fs_land[z] = fs[t]

    for j in range(ZN):

        @pl.when(jnp.logical_not(on_own & (z == j)))
        def _():
            rcopy(fs.at[0], fs_land.at[j], f_s.at[0], f_r.at[j], dp, mate).wait_recv()

    final = fs_land[0]
    for j in range(1, ZN):
        final = final + fs_land[j]
    og_ref[...] = final[0:COLS, :]

    for k in range(1, SEQ):
        x_copy(k, s).wait_send()
        a_copy(0, s, k).wait_send()
    for k in range(1, ZN):
        w1_copy(k).wait_send()

    @pl.when(jnp.logical_not(on_own))
    def _():
        w1_copy(0).wait_send()

    for k in range(1, XN):
        w2_copy(k, None).wait_send()
        w3_copy(k, None).wait_send()
        ya_copy(k).wait_send()
        xb_copy(k).wait_send()
        ax_copy(k).wait_send()
        by_copy(k).wait_send()
    for k in range(YN):
        w4_copy(k, c).wait_send()
        m_copy(k, c).wait_send()
    pair.wait_send()
    for t in range(SEQ):

        @pl.when(jnp.logical_not(on_own & (s == t)))
        def _():
            f_copy(t).wait_send()


def per_device(
    patches,
    segment_ids,
    regroup_plan,
    input_weight,
    input_bias,
    skip_weight,
    hidden_weight,
    output_bias,
    norm_gain,
    head_scale,
    qkv_weight,
    out_weight,
    cotangent,
):
    vmem = pl.BlockSpec(memory_space=pltpu.VMEM)
    smem = pl.BlockSpec(memory_space=pltpu.SMEM)
    hbm = pl.BlockSpec(memory_space=pl.ANY)
    dma = pltpu.SemaphoreType.DMA
    scratch = [
        pltpu.VMEM((D, D), BF),
        pltpu.VMEM((3, D, HW), BF),
        pltpu.VMEM((ROWS, D), BF),
        pltpu.VMEM((2, HW, ROWS), BF),
        pltpu.VMEM((SEQ * PATCH, ROWS), BF),
        pltpu.VMEM((SEQ * PATCH, D), BF),
        pltpu.VMEM((SEQ * PATCH, D), BF),
        pltpu.VMEM((D, 6 * LANES), BF),
        pltpu.VMEM((WIN, 3 * LANES), BF),
        pltpu.VMEM((4, ROWS, 3 * LANES), BF),
        pltpu.VMEM((ROWS, D), BF),
        pltpu.VMEM((8, HW), F32),
        pltpu.VMEM((SEQ, 8, HW), F32),
        pltpu.VMEM((XN, 48, HW), BF),
        pltpu.VMEM((D, HW), BF),
        pltpu.VMEM((SEQ, HD, ROWS), BF),
        pltpu.VMEM((HW, ROWS), BF),
        pltpu.VMEM((HW, HW), F32),
        pltpu.VMEM((HW, HW), F32),
        pltpu.VMEM((HW, HW), F32),
        pltpu.VMEM((YN, 160, ROWS), BF),
        pltpu.VMEM((YN, 160, ROWS), BF),
        pltpu.VMEM((XN, YN, 48, HW - ROWS), BF),
        pltpu.VMEM((XN, YN, 48, HW - ROWS), BF),
        pltpu.VMEM((XN, 48, ROWS), BF),
        pltpu.VMEM((XN, 48, ROWS), BF),
        pltpu.VMEM((YN, 48, HW - ROWS), BF),
        pltpu.VMEM((YN, 48, HW - ROWS), BF),
        pltpu.VMEM((GROUP, HW), F32),
        pltpu.VMEM((SEQ, 8, HW), F32),
        pltpu.VMEM((ZN, 8, HW), F32),
        dma((3,)),
        dma((8,)),
        dma((8,)),
        dma((8,)),
        dma((8,)),
        dma((4,)),
        dma((4,)),
        dma((4,)),
        dma((4,)),
        dma((4,)),
        dma((4,)),
        dma((4,)),
        dma((4,)),
        dma((8,)),
        dma((8,)),
        dma((1,)),
        dma((1,)),
        dma((4,)),
        dma((4,)),
        dma((4,)),
        dma((4,)),
        dma((4,)),
        dma((4,)),
        dma((4,)),
        dma((4,)),
        dma((8,)),
        dma((8,)),
    ]
    layer_out, grad = pl.pallas_call(
        whole_layer,
        out_shape=(
            jax.ShapeDtypeStruct((ROWS, D), BF),
            jax.ShapeDtypeStruct((COLS, HW), F32),
        ),
        in_specs=[vmem, vmem, vmem, vmem, vmem, vmem, hbm, vmem, vmem, smem, hbm, vmem, hbm],
        out_specs=(vmem, vmem),
        scratch_shapes=scratch,
        compiler_params=pltpu.CompilerParams(
            collective_id=0, has_side_effects=True, vmem_limit_bytes=50 * 1024 * 1024
        ),
        name="whole_layer",
    )(
        patches,
        segment_ids,
        jnp.transpose(regroup_plan, (1, 0, 2)),
        input_weight,
        input_bias.reshape(1, -1),
        skip_weight,
        hidden_weight,
        output_bias.reshape(1, -1),
        norm_gain.reshape(1, -1),
        head_scale,
        jnp.transpose(qkv_weight, (1, 0, 2)),
        jnp.transpose(out_weight),
        cotangent,
    )
    return layer_out, jnp.transpose(grad)


def solution(mesh):
    placed = (
        P(None, ("dp", "seq")),
        P("dp", None),
        P("dp", None, None),
        P(),
        P(),
        P(),
        P(),
        P(),
        P(),
        P(),
        P(),
        P(None, ("dp", "seq")),
        P(("dp", "seq"), None),
    )
    return jax.shard_map(
        per_device,
        mesh=mesh,
        in_specs=placed,
        out_specs=(P(("dp", "seq"), None), P(None, ("dp", "seq"))),
        check_vma=False,
    )
```

time: 474 us -> 89.7 us (0.19)
  waiting for transfers between devices: 342 us -> 0 us
  Pallas kernels: 0 us -> 78 us
  local copies, waits for them, and re-layouts: 52.6 us -> 10.1 us
  matrix products: 32.7 us -> 0 us
  between operations: 15 us -> 0.65 us
  starting transfers between devices: 12.9 us -> 0 us
  blocking collectives: 12.3 us -> 0 us
    unnamed x3 -> x0, waiting for transfers between devices: 261 us -> none
    pallas_call x0 -> x1, Pallas kernels: none -> 78 us  [per_device(): pl.pallas_call(whole_layer, out_shape=(jax.ShapeDtypeStruct((ROWS, D), BF...]
    all_gather x1 -> x0, waiting for transfers between devices: 53.6 us -> none  [per_device(): lax.all_gather(out_weight, ('dp', 'seq'), axis=1, tiled=True)]
    dot_general x17 -> x0, matrix products: 32.7 us -> none  [the longest x6 9.7 us: per_device(): jnp.einsum('qhd,khd->hqk', query_part, key_part, preferred_element_type=j...]
    all_to_all x2 -> x0, waiting for transfers between devices: 27.5 us -> none  [the longest x1 22.7 us: per_device(): lax.all_to_all(projected, 'seq', split_axis=2, concat_axis=0, tiled=True)]
    scatter x2 -> x0, local copies, waits for them, and re-layouts: 14.9 us -> none  [the longest x1 11.9 us: per_device(): receive_table = jnp.zeros((shard_rows,), jnp.int32).at[landing].set(loade...]
    all_to_all x2 -> x0, starting transfers between devices: 12.7 us -> none  [the longest x1 7.46 us: per_device(): lax.all_to_all(padded[send_table], 'seq', split_axis=0, concat_axis=0, ti...]
    all_to_all x1 -> x0, blocking collectives: 12.3 us -> none  [per_device(): lax.all_to_all(attended, 'seq', split_axis=0, concat_axis=1, tiled=True)]
  transfers between devices with their start and end apart: 4 -> 0, of which waited for: 4 -> 0; matrix products, arithmetic and copies ran while one was open for 10% -> 0% of each run, Pallas kernels for 0% -> 0%
where the time goes in v1:
time: 89.7 us; the launch traced here: 88.7 us
  Pallas kernels  78 us (87%)
  local copies, waits for them, and re-layouts  10.1 us (11%)
    pallas_call x1, Pallas kernels, per_device(): pl.pallas_call(whole_layer, out_shape=(jax.ShapeDtypeStruct((ROWS, D), BF...  78 us
    unnamed x18, local copies, waits for them, and re-layouts  8.01 us

profile of v1, /device:TPU:1, one launch (start us, length us, event | category | flops | bytes accessed | tf_op | source)
XLA Modules:
  0.0 88.7 jit_solution(2054549886712449509)
XLA Ops:
  0.6 0.7 reshape.13.bin_ref
  1.3 0.7 reshape.14.ob_ref
  2.0 0.7 reshape.15.gain_ref
  2.7 0.0 copy-start
  2.7 1.2 %copy-done = bf16[384,1280]{1,0:T(8,128)(2,1)S(1)} copy-done((bf16[384,1280]{1,0:T(8,128)(2,1)S(1)}, bf16[384,1280]{1,0:T(8,128)(2,1)}, u32[]{:S(2)}) %copy-start) | copy-done | bytes 983064
  3.9 0.0 copy-start.1
  3.9 0.9 copy-done.1
  4.8 0.0 copy-start.2
  4.8 0.9 copy-done.2
  5.7 0.0 copy-start.3
  5.7 0.7 copy-done.3
  6.4 0.0 copy-start.4
  6.5 0.7 copy-done.4
  7.2 0.0 copy-start.5
  7.2 0.7 copy-done.5
  7.9 0.0 copy-start.6
  7.9 0.7 copy-done.6
  8.5 0.0 copy-start.7
  8.5 0.7 copy-done.7
  9.2 78.0 %whole_layer.1 = (bf16[384,1280]{1,0:T(8,128)(2,1)S(1)}, f32[5,640]{1,0:T(8,128)S(1)}) custom-call(bf16[32,384]{1,0:T(8,128)(2,1)S(1)} %copy-done.3, s32[1,3072]{1,0:T(1,128)S(1)} %copy-done.4, s32[5,1,64]{2,1,0:T(1,128)S(1)} %bitcast.6, bf16[32,1280]{1,0:T(8,128)(2,1)S(1)} %copy-done.1, f32[1,1280]{1,0:T(1,128)S(1)} %reshape.13.bin_ref, ...), custom_call_target="tpu_custom_call" | custom-call | tf_op jit(solution)/shard_map/whole_layer/pallas_call | solution.py:601
  87.2 0.9 %copy.17 = bf16[384,1280]{1,0:T(8,128)(2,1)} copy(bf16[384,1280]{1,0:T(8,128)(2,1)S(1)} %get-tuple-element.8) | data formatting | bytes 1966080
  88.1 0.6 copy.18
Async XLA Ops:
  2.7 1.2 %copy-start = (bf16[384,1280]{1,0:T(8,128)(2,1)S(1)}, bf16[384,1280]{1,0:T(8,128)(2,1)}, u32[]{:S(2)}) copy-start(bf16[384,1280]{1,0:T(8,128)(2,1)} %cot_hbm.1) | copy-start | bytes 2949124
  3.9 0.9 copy-start.1
  4.8 0.9 copy-start.2
  5.7 0.7 copy-start.3
  6.4 0.7 copy-start.4
  7.2 0.7 copy-start.5
  7.9 0.7 copy-start.6
  8.5 0.7 copy-start.7

commit v2 on v1

--- a/solution.py
+++ b/solution.py
@@ -41,24 +41,35 @@
 
 
 def whole_layer(
+    x_hbm,
+    seg_hbm,
+    plan_hbm,
+    win_hbm,
+    bin_hbm,
+    wskip_hbm,
+    wh_hbm,
+    ob_hbm,
+    gain_hbm,
+    hs_hbm,
+    qkvw_hbm,
+    ow_hbm,
+    cot_hbm,
+    lo_ref,
+    og_ref,
     x_ref,
     seg_ref,
     plan_ref,
     win_ref,
     bin_ref,
     wskip_ref,
-    wh_hbm,
     ob_ref,
     gain_ref,
     hs_ref,
-    qkvw_hbm,
     ow_ref,
-    cot_hbm,
-    lo_ref,
-    og_ref,
     wh,
     qkvw,
     cot,
+    cot_f,
     cot_t,
     xg,
     win8,
@@ -71,6 +82,8 @@
     w_land,
     wx,
     wt,
+    wt_f,
+    tiles,
     att_send,
     ret,
     p_own,
@@ -85,6 +98,7 @@
     by,
     by_land,
     block40,
+    fs_f,
     fs,
     fs_land,
     ld_sem,
@@ -122,10 +136,6 @@
     y = s // 2
     c = s % 2
     mate = y * 2 + (1 - c)
-    zmine = c * YN + y
-    ownseq = (z % YN) * 2 + z // YN
-    on_own = z == zmine
-
     def rcopy(src, dst, ssem, rsem, dp_t, seq_t):
         return pltpu.make_async_remote_copy(
             src_ref=src,
@@ -140,9 +150,24 @@
         return zz * XN + x2
 
     loads = [
-        pltpu.make_async_copy(qkvw_hbm, qkvw, ld_sem.at[0]),
-        pltpu.make_async_copy(wh_hbm, wh, ld_sem.at[1]),
-        pltpu.make_async_copy(cot_hbm, cot, ld_sem.at[2]),
+        pltpu.make_async_copy(src, dst, ld_sem.at[i])
+        for i, (src, dst) in enumerate(
+            [
+                (x_hbm, x_ref),
+                (ow_hbm, ow_ref),
+                (win_hbm, win_ref),
+                (wskip_hbm, wskip_ref),
+                (qkvw_hbm.at[:, :, pl.ds(pl.multiple_of(y * LANES, LANES), 2 * LANES)], qkvw),
+                (plan_hbm, plan_ref),
+                (seg_hbm, seg_ref),
+                (bin_hbm, bin_ref),
+                (ob_hbm, ob_ref),
+                (gain_hbm, gain_ref),
+                (hs_hbm, hs_ref),
+                (wh_hbm, wh),
+                (cot_hbm, cot),
+            ]
+        )
     ]
     for ld in loads:
         ld.start()
@@ -157,18 +182,10 @@
     for k in range(1, XN):
         greet(dpi(z, (xx + k) % XN), s)
     for k in range(1, ZN):
-        greet(dpi((z + k) % ZN, xx), ownseq)
-
-    @pl.when(jnp.logical_not(on_own))
-    def _():
-        greet(dp, ownseq)
-
-    for t in range(SEQ):
-
-        @pl.when(jnp.logical_not(on_own & (s == t)))
-        def _():
-            greet(dpi(zmine, xx), jnp.int32(t))
-
+        greet(dpi((z + k) % ZN, xx), s)
+
+    for ld in loads[:4]:
+        ld.wait()
     ow_send[...] = jnp.zeros((8, HW), F32)
     ow_send[0:COLS, :] = ow_ref[...].astype(F32)
     for k in range(SEQ):
@@ -176,7 +193,7 @@
         wskip8[k * PATCH : (k + 1) * PATCH, :] = wskip_ref[...]
     xg[pl.ds(pl.multiple_of(s * PATCH, PATCH), PATCH), :] = x_ref[...]
 
-    pl.semaphore_wait(bar, 7 + 3 + 16 - 2 * on_own.astype(jnp.int32))
+    pl.semaphore_wait(bar, 7 + 3 + 7)
 
     def x_copy(k, source):
         rows = xg.at[pl.ds(pl.multiple_of(source * PATCH, PATCH), PATCH), :]
@@ -185,25 +202,17 @@
     for k in range(1, SEQ):
         x_copy(k, s).start()
 
-    def w1_copy(k):
-        return rcopy(
-            ow_send, w_land.at[s], w1_s.at[k], w1_r.at[s], dpi((z + k) % ZN, xx), ownseq
-        )
+    def w1_copy(k, source):
+        slot = w_land.at[pl.ds(pl.multiple_of(source * 8, 8), 8), :]
+        return rcopy(ow_send, slot, w1_s.at[k], w1_r.at[k], dpi((z + k) % ZN, xx), s)
 
     for k in range(1, ZN):
-        w1_copy(k).start()
-
-    @pl.when(jnp.logical_not(on_own))
-    def _():
-        w1_copy(0).start()
-
-    @pl.when(on_own)
-    def _():
-        w_land[s] = ow_send[...]
-
-    loads[0].wait()
-    feature = iota((HW, 2 * LANES), 0)
-    lane2 = iota((HW, 2 * LANES), 1)
+        w1_copy(k, z).start()
+    w_land[pl.ds(pl.multiple_of(z * 8, 8), 8), :] = ow_send[...]
+
+    loads[4].wait()
+    feature = iota((2 * LANES, 2 * LANES), 0) + y * LANES
+    lane2 = iota((2 * LANES, 2 * LANES), 1)
     inner = lane2 % LANES
     head = jnp.where(lane2 < LANES, s, mate)
     pick = jnp.where((inner < HD) & (feature == head * HD + inner), 1.0, 0.0).astype(BF)
@@ -218,10 +227,8 @@
 
         lax.fori_loop(0, D // 256, pick_rows, 0)
 
-    loads[2].wait()
-    for i in range(2):
-        cot_t[i] = jnp.transpose(cot[:, i * HW : (i + 1) * HW])
-    loads[1].wait()
+    for ld in loads[5:12]:
+        ld.wait()
     for k in range(1, SEQ):
         x_copy(k, (s - k + SEQ) % SEQ).wait_recv()
 
@@ -238,17 +245,12 @@
     def wt_rows(zz):
         return wt.at[pl.ds(pl.multiple_of(zz * 160, 32), 160), :]
 
-    def zof(seq):
-        return (seq % 2) * YN + seq // 2
-
     def w3_copy(k, source):
-        block = zof(s) if source is None else zof(source)
-        return rcopy(
-            wt_rows(zof(s)), wt_rows(block), w3_s.at[k], w3_r.at[k], dp, ((y + k) % YN) * 2 + c
-        )
+        block = wt_rows(source)
+        return rcopy(block, block, w3_s.at[k], w3_r.at[k], dp, ((y + k) % YN) * 2 + c)
 
     def w4_copy(k, core):
-        block = wt_rows(core * YN + (y - k + YN) % YN)
+        block = wt_rows(((y - k + YN) % YN) * 2 + core)
         return rcopy(block, block, w4_s.at[k], w4_r.at[k], dp, mate)
 
     def m_copy(i, core):
@@ -258,7 +260,7 @@
     lane = iota((ROWS, LANES), 1)
     seg_lane = (lane >= HD) & (lane < HD + 16)
 
-    def embed_chunk(i, carry):
+    def embed_chunk(i):
         chunk = 2 * i + c
         first_row = pl.multiple_of(chunk * ROWS, ROWS)
         pos = first_row + iota((ROWS, 64), 0)
@@ -274,17 +276,15 @@
         cols = jnp.where(
             iota((ROWS, SEQ * PATCH), 1) // PATCH == shard_of, spread, 0.0
         ).astype(BF)
-        half = (dot(cols, win8[...]) + bin_ref[...]) * 0.5
+        half = (dot(cols, win8[...]) + bin_ref[...].reshape(1, D)) * 0.5
         hidden = (half + half * jnp.tanh(half)).astype(BF)
-        emb = (dot(hidden, wh[...]) + dot(cols, wskip8[...]) + ob_ref[...]).astype(BF)
-
-        @pl.when(i == y)
-        def _():
-            emb_own[...] = emb
+        emb = (dot(hidden, wh[...]) + dot(cols, wskip8[...]) + ob_ref[...].reshape(1, D)).astype(BF)
+
+        emb_own[i] = emb
 
         wide = emb.astype(F32)
         scale = lax.rsqrt(jnp.mean(wide * wide, axis=-1, keepdims=True) + EPS)
-        normed = (wide * scale * gain_ref[...]).astype(BF)
+        normed = (wide * scale * gain_ref[...].reshape(1, D)).astype(BF)
         proj = dot(normed, wsel[...]).astype(BF)
 
         seg_row = seg_ref[:, pl.ds(first_row, ROWS)]
@@ -306,37 +306,32 @@
         for j in range(3):
             qkv[pl.ds(first_row, ROWS), j * LANES : (j + 1) * LANES] = parts[0][j]
 
-        @pl.when(i == 0)
-        def _():
-            for t in range(SEQ):
-
-                @pl.when(jnp.logical_not(on_own & (s == t)))
-                def _():
-                    rcopy(ow_send, w_land.at[t], w1_s.at[0], w1_r.at[t], dp, mate).wait_recv()
-
-            block = jnp.concatenate([w_land[t, 0:COLS, :] for t in range(SEQ)], axis=0)
-            block = jnp.concatenate([block, jnp.zeros((8, HW), F32)], axis=0)
-            wx[xx] = block.astype(BF)
-            for k in range(1, XN):
-                w2_copy(k, None).start()
-
-        @pl.when(i == 1)
-        def _():
-            for k in range(1, XN):
-                w2_copy(k, (xx - k + XN) % XN).wait_recv()
-            block = jnp.concatenate([wx[j, 0:GROUP, :].astype(F32) for j in range(XN)], axis=0)
-            wt[pl.ds(pl.multiple_of(zmine * 160, 32), 160), :] = block.astype(BF)
-            for k in range(1, YN):
-                w3_copy(k, None).start()
-            w4_copy(0, c).start()
-
-        return carry
-
-    lax.fori_loop(0, 4, embed_chunk, 0)
-
+    embed_chunk(0)
+    for k in range(1, ZN):
+        w1_copy(k, (z - k + ZN) % ZN).wait_recv()
+    for m in range(5):
+        tiles[m] = w_land[:, m * LANES : (m + 1) * LANES]
+    block = jnp.concatenate(
+        [
+            jnp.concatenate([tiles[m, pl.ds(j, ZN, stride=8), :] for j in range(COLS)], axis=0)
+            for m in range(5)
+        ],
+        axis=1,
+    )
+    block = jnp.concatenate([block, jnp.zeros((8, HW), F32)], axis=0)
+    wx[xx] = block.astype(BF)
+    for k in range(1, XN):
+        w2_copy(k, None).start()
+    embed_chunk(1)
+    for k in range(1, XN):
+        w2_copy(k, (xx - k + XN) % XN).wait_recv()
+    block = jnp.concatenate([wx[j, 0:GROUP, :].astype(F32) for j in range(XN)], axis=0)
+    wt[pl.ds(pl.multiple_of(s * 160, 32), 160), :] = block.astype(BF)
     for k in range(1, YN):
-        w3_copy(k, ((y - k + YN) % YN) * 2 + c).wait_recv()
-        w4_copy(k, c).start()
+        w3_copy(k, s).start()
+    w4_copy(0, c).start()
+    embed_chunk(2)
+    embed_chunk(3)
     for i in range(4):
         m_copy(i, 1 - c).wait_recv()
 
@@ -370,24 +365,49 @@
         def _():
             a_copy(b, s, (b - s + SEQ) % SEQ).start()
 
+        if b == 3:
+            for k in range(1, YN):
+                w3_copy(k, ((y - k + YN) % YN) * 2 + c).wait_recv()
+                w4_copy(k, c).start()
+
+    loads[12].wait()
+    for m in range(3):
+        cot_f[m] = jnp.transpose(cot[m * LANES : (m + 1) * LANES, :].astype(F32))
+    for core in range(2):
+        for j in range(YN):
+            base = [x2 * GROUP + (2 * j + core) * COLS + n for x2 in range(XN) for n in range(COLS)]
+            for m in range(3):
+                rows = [cot_f[m, pl.ds(first, ZN, stride=160), :] for first in base]
+                rows = jnp.concatenate(rows, axis=0).astype(BF)
+                cot_t[core, j * 160 : (j + 1) * 160, m * LANES : (m + 1) * LANES] = rows
+    for k in range(YN):
+        w4_copy(k, 1 - c).wait_recv()
+    for t in range(SEQ):
+        block = wt[t * 160 : (t + 1) * 160, :].astype(F32)
+        for x2 in range(XN):
+            for n in range(COLS):
+                first = x2 * GROUP + n * ZN
+                rows = pl.ds(x2 * GROUP + t * COLS + n, ZN, stride=160)
+                for m in range(5):
+                    wt_f[m, rows, :] = block[first : first + ZN, m * LANES : (m + 1) * LANES]
+
     for k in range(1, SEQ):
         a_copy(0, (s - k + SEQ) % SEQ, k).wait_recv()
 
     attended = ret[...]
-    p_send[...] = dot_nt(cot_t[1 - c], attended)
-    pair = rcopy(p_send, p_land, p_s.at[0], p_r.at[0], dp, mate)
-    pair.start()
+    order = [2, 1, 3, 0]
+
+    def p_copy(k):
+        piece = (y + k) % YN
+        return rcopy(p_send.at[piece], p_land.at[piece], p_s.at[k], p_r.at[k], dp, mate)
+
+    def owner_rows(k):
+        return pl.ds(pl.multiple_of(((y + k) % YN) * 160, 32), 160)
+
+    for k in order:
+        p_send[(y + k) % YN] = dot_nt(cot_t[1 - c, owner_rows(k), :], attended).astype(BF)
+        p_copy(k).start()
     p_own[...] = dot_nt(cot_t[c], attended)
-
-    pair.wait_recv()
-    summed = p_own[...] + p_land[...]
-    p_own[...] = summed
-    half_rows = summed.reshape(YN, XN, GROUP, HW)
-    for j in range(YN):
-        ya[j] = summed[j * 160 : (j + 1) * 160, 0:ROWS].astype(BF)
-    pad = jnp.zeros((YN, 8, HW - ROWS), F32)
-    for j in range(XN):
-        xb[j] = jnp.concatenate([half_rows[:, j, :, ROWS:], pad], axis=1).astype(BF)
 
     def ya_copy(k):
         to = (y + k) % YN
@@ -397,17 +417,27 @@
         to = (xx + k) % XN
         return rcopy(xb.at[to], xb_land.at[k], xb_s.at[k], xb_r.at[k], dpi(z, to), s)
 
-    for k in range(1, YN):
-        ya_copy(k).start()
+    pad = jnp.zeros((8, HW - ROWS), F32)
+    for k in order:
+        to = (y + k) % YN
+        p_copy(k).wait_recv()
+        piece = p_own[owner_rows(k), :] + p_land[to].astype(F32)
+        p_own[owner_rows(k), :] = piece
+        if k:
+            ya[to] = piece[:, 0:ROWS].astype(BF)
+            ya_copy(k).start()
+        for j in range(XN):
+            part = piece[j * GROUP : (j + 1) * GROUP, ROWS:]
+            xb[j, to] = jnp.concatenate([part, pad], axis=0).astype(BF)
+    for k in (2, 1, 3):
         xb_copy(k).start()
 
-    for k in range(YN):
-        w4_copy(k, 1 - c).wait_recv()
     rows = jnp.transpose(attended)
     for j in range(5):
         cols = slice(j * 256, (j + 1) * 256)
-        branch = dot_nt(rows, wt[cols, :])
-        lo_ref[:, cols] = (emb_own[:, cols].astype(F32) + branch).astype(BF)
+        weight = jnp.concatenate([wt_f[m, cols, :].astype(BF) for m in range(5)], axis=1)
+        branch = dot_nt(rows, weight)
+        lo_ref[:, cols] = (emb_own[y, :, cols].astype(F32) + branch).astype(BF)
 
     for k in range(1, YN):
         ya_copy(k).wait_recv()
@@ -463,47 +493,37 @@
         right = right + by_land[k].astype(F32)[0:GROUP, :]
     block40[:, 0:ROWS] = left
     block40[:, ROWS:HW] = right
-    fs[...] = jnp.zeros_like(fs)
-    for t in range(SEQ):
-        fs[t, 0:COLS, :] = block40[t * COLS : (t + 1) * COLS, :]
-
-    def f_copy(t):
-        return rcopy(fs.at[t], fs_land.at[z], f_s.at[t], f_r.at[z], dpi(zmine, xx), jnp.int32(t))
-
-    for t in range(SEQ):
-
-        @pl.when(jnp.logical_not(on_own & (s == t)))
-        def _():
-            f_copy(t).start()
-
-        @pl.when(on_own & (s == t))
-        def _():
-            fs_land[z] = fs[t]
-
+    for m in range(5):
+        tiles[m, 0:GROUP, :] = block40[:, m * LANES : (m + 1) * LANES]
     for j in range(ZN):
-
-        @pl.when(jnp.logical_not(on_own & (z == j)))
-        def _():
-            rcopy(fs.at[0], fs_land.at[j], f_s.at[0], f_r.at[j], dp, mate).wait_recv()
-
-    final = fs_land[0]
-    for j in range(1, ZN):
-        final = final + fs_land[j]
-    og_ref[...] = final[0:COLS, :]
+        for m in range(5):
+            part = tiles[m, pl.ds(j, COLS, stride=ZN), :]
+            fs_f[j, m * COLS : (m + 1) * COLS, :] = part
+    fs[...] = fs_f[...].astype(BF)
+
+    def f_copy(k):
+        to = (z + k) % ZN
+        return rcopy(fs.at[to], fs_land.at[k], f_s.at[k], f_r.at[k], dpi(to, xx), s)
+
+    for k in (4, 3, 5, 2, 6, 1, 7):
+        f_copy(k).start()
+    final = fs_f[z]
+    for k in range(1, ZN):
+        f_copy(k).wait_recv()
+        final = final + fs_land[k].astype(F32)
+    fs_f[0] = final
+    for m in range(COLS):
+        og_ref[:, m * LANES : (m + 1) * LANES] = fs_f[0, m * COLS : (m + 1) * COLS, :]
 
     for k in range(1, SEQ):
         x_copy(k, s).wait_send()
         a_copy(0, s, k).wait_send()
     for k in range(1, ZN):
-        w1_copy(k).wait_send()
-
-    @pl.when(jnp.logical_not(on_own))
-    def _():
-        w1_copy(0).wait_send()
-
+        w1_copy(k, z).wait_send()
+        f_copy(k).wait_send()
     for k in range(1, XN):
         w2_copy(k, None).wait_send()
-        w3_copy(k, None).wait_send()
+        w3_copy(k, s).wait_send()
         ya_copy(k).wait_send()
         xb_copy(k).wait_send()
         ax_copy(k).wait_send()
@@ -511,12 +531,7 @@
     for k in range(YN):
         w4_copy(k, c).wait_send()
         m_copy(k, c).wait_send()
-    pair.wait_send()
-    for t in range(SEQ):
-
-        @pl.when(jnp.logical_not(on_own & (s == t)))
-        def _():
-            f_copy(t).wait_send()
+        p_copy(k).wait_send()
 
 
 def per_device(
@@ -535,13 +550,23 @@
     cotangent,
 ):
     vmem = pl.BlockSpec(memory_space=pltpu.VMEM)
-    smem = pl.BlockSpec(memory_space=pltpu.SMEM)
-    hbm = pl.BlockSpec(memory_space=pl.ANY)
+    hbm = pl.BlockSpec(memory_space=pltpu.HBM)
     dma = pltpu.SemaphoreType.DMA
     scratch = [
+        pltpu.VMEM((PATCH, ROWS), BF),
+        pltpu.VMEM((1, WIN), jnp.int32),
+        pltpu.VMEM((5, 1, 64), jnp.int32),
+        pltpu.VMEM((PATCH, D), BF),
+        pltpu.VMEM((D,), F32),
+        pltpu.VMEM((PATCH, D), BF),
+        pltpu.VMEM((D,), F32),
+        pltpu.VMEM((D,), F32),
+        pltpu.SMEM((SEQ,), F32),
+        pltpu.VMEM((COLS, HW), BF),
         pltpu.VMEM((D, D), BF),
-        pltpu.VMEM((3, D, HW), BF),
+        pltpu.VMEM((3, D, 2 * LANES), BF),
         pltpu.VMEM((ROWS, D), BF),
+        pltpu.VMEM((3, D, LANES), F32),
         pltpu.VMEM((2, HW, ROWS), BF),
         pltpu.VMEM((SEQ * PATCH, ROWS), BF),
         pltpu.VMEM((SEQ * PATCH, D), BF),
@@ -549,16 +574,18 @@
         pltpu.VMEM((D, 6 * LANES), BF),
         pltpu.VMEM((WIN, 3 * LANES), BF),
         pltpu.VMEM((4, ROWS, 3 * LANES), BF),
-        pltpu.VMEM((ROWS, D), BF),
+        pltpu.VMEM((4, ROWS, D), BF),
         pltpu.VMEM((8, HW), F32),
-        pltpu.VMEM((SEQ, 8, HW), F32),
+        pltpu.VMEM((ZN * 8, HW), F32),
         pltpu.VMEM((XN, 48, HW), BF),
         pltpu.VMEM((D, HW), BF),
+        pltpu.VMEM((5, D, LANES), F32),
+        pltpu.VMEM((5, 64, LANES), F32),
         pltpu.VMEM((SEQ, HD, ROWS), BF),
         pltpu.VMEM((HW, ROWS), BF),
         pltpu.VMEM((HW, HW), F32),
-        pltpu.VMEM((HW, HW), F32),
-        pltpu.VMEM((HW, HW), F32),
+        pltpu.VMEM((YN, 160, HW), BF),
+        pltpu.VMEM((YN, 160, HW), BF),
         pltpu.VMEM((YN, 160, ROWS), BF),
         pltpu.VMEM((YN, 160, ROWS), BF),
         pltpu.VMEM((XN, YN, 48, HW - ROWS), BF),
@@ -568,25 +595,26 @@
         pltpu.VMEM((YN, 48, HW - ROWS), BF),
         pltpu.VMEM((YN, 48, HW - ROWS), BF),
         pltpu.VMEM((GROUP, HW), F32),
-        pltpu.VMEM((SEQ, 8, HW), F32),
-        pltpu.VMEM((ZN, 8, HW), F32),
-        dma((3,)),
-        dma((8,)),
-        dma((8,)),
-        dma((8,)),
-        dma((8,)),
-        dma((4,)),
-        dma((4,)),
-        dma((4,)),
-        dma((4,)),
-        dma((4,)),
-        dma((4,)),
-        dma((4,)),
-        dma((4,)),
-        dma((8,)),
-        dma((8,)),
-        dma((1,)),
-        dma((1,)),
+        pltpu.VMEM((ZN, 32, LANES), F32),
+        pltpu.VMEM((ZN, 32, LANES), BF),
+        pltpu.VMEM((ZN, 32, LANES), BF),
+        dma((13,)),
+        dma((8,)),
+        dma((8,)),
+        dma((8,)),
+        dma((8,)),
+        dma((4,)),
+        dma((4,)),
+        dma((4,)),
+        dma((4,)),
+        dma((4,)),
+        dma((4,)),
+        dma((4,)),
+        dma((4,)),
+        dma((8,)),
+        dma((8,)),
+        dma((4,)),
+        dma((4,)),
         dma((4,)),
         dma((4,)),
         dma((4,)),
@@ -604,11 +632,11 @@
             jax.ShapeDtypeStruct((ROWS, D), BF),
             jax.ShapeDtypeStruct((COLS, HW), F32),
         ),
-        in_specs=[vmem, vmem, vmem, vmem, vmem, vmem, hbm, vmem, vmem, smem, hbm, vmem, hbm],
+        in_specs=[hbm] * 13,
         out_specs=(vmem, vmem),
         scratch_shapes=scratch,
         compiler_params=pltpu.CompilerParams(
-            collective_id=0, has_side_effects=True, vmem_limit_bytes=50 * 1024 * 1024
+            collective_id=0, has_side_effects=True, vmem_limit_bytes=63 * 1024 * 1024
         ),
         name="whole_layer",
     )(
@@ -616,11 +644,11 @@
         segment_ids,
         jnp.transpose(regroup_plan, (1, 0, 2)),
         input_weight,
-        input_bias.reshape(1, -1),
+        input_bias,
         skip_weight,
         hidden_weight,
-        output_bias.reshape(1, -1),
-        norm_gain.reshape(1, -1),
+        output_bias,
+        norm_gain,
         head_scale,
         jnp.transpose(qkv_weight, (1, 0, 2)),
         jnp.transpose(out_weight),

time: 89.7 us -> 72.9 us (0.81)
  Pallas kernels: 78 us -> 67.6 us
  local copies, waits for them, and re-layouts: 10.1 us -> 3.54 us
    pallas_call x1, Pallas kernels: 78 us -> 67.6 us  [per_device(): pl.pallas_call(whole_layer, out_shape=(jax.ShapeDtypeStruct((ROWS, D), BF...]
    unnamed x18 -> x2, local copies, waits for them, and re-layouts: 8.01 us -> 3.54 us
    reshape x3 -> x0, local copies, waits for them, and re-layouts: 2.1 us -> none  [the longest x1 0.7 us: per_device(): input_bias.reshape(1, -1)]
where the time goes in v2:
time: 72.9 us; the launch traced here: 71.8 us
  Pallas kernels  67.6 us (93%)
  local copies, waits for them, and re-layouts  3.54 us (5%)
    pallas_call x1, Pallas kernels, per_device(): pl.pallas_call(whole_layer, out_shape=(jax.ShapeDtypeStruct((ROWS, D), BF...  67.6 us
    unnamed x2, local copies, waits for them, and re-layouts  3.54 us

profile of v2, /device:TPU:1, one launch (start us, length us, event | category | flops | bytes accessed | tf_op | source)
XLA Modules:
  0.0 71.8 jit_solution(8065559277977228355)
XLA Ops:
  0.6 67.6 %whole_layer.1 = (bf16[384,1280]{1,0:T(8,128)(2,1)}, f32[5,640]{1,0:T(8,128)}) custom-call(bf16[32,384]{1,0:T(8,128)(2,1)} %x_hbm.1, s32[1,3072]{1,0:T(1,128)} %seg_hbm.1, s32[5,1,64]{2,1,0:T(1,128)} %bitcast.7, bf16[32,1280]{1,0:T(8,128)(2,1)} %win_hbm.1, f32[1280]{0:T(1024)} %bin_hbm.1, bf16[32,1280]{1,0:T(8,128)(2,1)} %wskip_hbm.1, ...), custom_call_target="tpu_custom_call" | custom-call | tf_op jit(solution)/shard_map/whole_layer/pallas_call | solution.py:629
  68.3 2.2 %copy.17 = bf16[384,1280]{1,0:T(8,128)(2,1)} copy(bf16[384,1280]{1,0:T(8,128)(2,1)} %get-tuple-element.8) | data formatting | bytes 1966080
  70.5 1.3 %copy.18 = f32[640,5]{0,1:T(8,128)} copy(f32[640,5]{0,1:T(8,128)} %bitcast.5) | data formatting | bytes 25600

commit v3 on v2

--- a/solution.py
+++ b/solution.py
@@ -56,7 +56,6 @@
     cot_hbm,
     lo_ref,
     og_ref,
-    x_ref,
     seg_ref,
     plan_ref,
     win_ref,
@@ -149,11 +148,23 @@
     def dpi(zz, x2):
         return zz * XN + x2
 
+    bar = pltpu.get_barrier_semaphore()
+
+    def greet(dp_t, seq_t):
+        pl.semaphore_signal(bar, inc=1, device_id=(dp_t, seq_t), device_id_type=MESH)
+
+    for k in range(1, SEQ):
+        greet(dp, (s + k) % SEQ)
+    for k in range(1, XN):
+        greet(dpi(z, (xx + k) % XN), s)
+    for k in range(1, ZN):
+        greet(dpi((z + k) % ZN, xx), s)
+
     loads = [
         pltpu.make_async_copy(src, dst, ld_sem.at[i])
         for i, (src, dst) in enumerate(
             [
-                (x_hbm, x_ref),
+                (x_hbm, xg.at[pl.ds(pl.multiple_of(s * PATCH, PATCH), PATCH), :]),
                 (ow_hbm, ow_ref),
                 (win_hbm, win_ref),
                 (wskip_hbm, wskip_ref),
@@ -172,43 +183,33 @@
     for ld in loads:
         ld.start()
 
-    bar = pltpu.get_barrier_semaphore()
-
-    def greet(dp_t, seq_t):
-        pl.semaphore_signal(bar, inc=1, device_id=(dp_t, seq_t), device_id_type=MESH)
+    pl.semaphore_wait(bar, 7 + 3 + 7)
+
+    def x_copy(k, source):
+        rows = xg.at[pl.ds(pl.multiple_of(source * PATCH, PATCH), PATCH), :]
+        return rcopy(x_hbm, rows, x_s.at[k], x_r.at[k], dp, (s + k) % SEQ)
 
     for k in range(1, SEQ):
-        greet(dp, (s + k) % SEQ)
-    for k in range(1, XN):
-        greet(dpi(z, (xx + k) % XN), s)
-    for k in range(1, ZN):
-        greet(dpi((z + k) % ZN, xx), s)
-
-    for ld in loads[:4]:
+        x_copy(k, s).start()
+
+    for ld in loads[1:2]:
         ld.wait()
     ow_send[...] = jnp.zeros((8, HW), F32)
     ow_send[0:COLS, :] = ow_ref[...].astype(F32)
+
+    def w1_copy(k, source):
+        slot = w_land.at[pl.ds(pl.multiple_of(source * 8, 8), 8), :]
+        return rcopy(ow_send, slot, w1_s.at[k], w1_r.at[k], dpi((z + k) % ZN, xx), s)
+
+    for k in range(1, ZN):
+        w1_copy(k, z).start()
+    w_land[pl.ds(pl.multiple_of(z * 8, 8), 8), :] = ow_send[...]
+
+    for ld in (loads[0], *loads[2:4]):
+        ld.wait()
     for k in range(SEQ):
         win8[k * PATCH : (k + 1) * PATCH, :] = win_ref[...]
         wskip8[k * PATCH : (k + 1) * PATCH, :] = wskip_ref[...]
-    xg[pl.ds(pl.multiple_of(s * PATCH, PATCH), PATCH), :] = x_ref[...]
-
-    pl.semaphore_wait(bar, 7 + 3 + 7)
-
-    def x_copy(k, source):
-        rows = xg.at[pl.ds(pl.multiple_of(source * PATCH, PATCH), PATCH), :]
-        return rcopy(x_ref, rows, x_s.at[k], x_r.at[k], dp, (s + k) % SEQ)
-
-    for k in range(1, SEQ):
-        x_copy(k, s).start()
-
-    def w1_copy(k, source):
-        slot = w_land.at[pl.ds(pl.multiple_of(source * 8, 8), 8), :]
-        return rcopy(ow_send, slot, w1_s.at[k], w1_r.at[k], dpi((z + k) % ZN, xx), s)
-
-    for k in range(1, ZN):
-        w1_copy(k, z).start()
-    w_land[pl.ds(pl.multiple_of(z * 8, 8), 8), :] = ow_send[...]
 
     loads[4].wait()
     feature = iota((2 * LANES, 2 * LANES), 0) + y * LANES
@@ -217,16 +218,9 @@
     head = jnp.where(lane2 < LANES, s, mate)
     pick = jnp.where((inner < HD) & (feature == head * HD + inner), 1.0, 0.0).astype(BF)
     for i in range(3):
-
-        def pick_rows(r, carry, i=i):
-            rows = pl.ds(pl.multiple_of(r * 256, 256), 256)
-            part = dot(qkvw[i, rows, :], pick).astype(BF)
-            wsel[rows, i * LANES : (i + 1) * LANES] = part[:, :LANES]
-            wsel[rows, (3 + i) * LANES : (4 + i) * LANES] = part[:, LANES:]
-            return carry
-
-        lax.fori_loop(0, D // 256, pick_rows, 0)
-
+        part = dot(qkvw[i], pick).astype(BF)
+        wsel[:, i * LANES : (i + 1) * LANES] = part[:, :LANES]
+        wsel[:, (3 + i) * LANES : (4 + i) * LANES] = part[:, LANES:]
     for ld in loads[5:12]:
         ld.wait()
     for k in range(1, SEQ):
@@ -257,13 +251,13 @@
         rows = pl.multiple_of((2 * i + core) * ROWS, ROWS)
         return rcopy(msend.at[i], qkv.at[pl.ds(rows, ROWS), :], m_s.at[i], m_r.at[i], dp, mate)
 
-    lane = iota((ROWS, LANES), 1)
+    lane = iota((2 * ROWS, LANES), 1)
     seg_lane = (lane >= HD) & (lane < HD + 16)
 
-    def embed_chunk(i):
-        chunk = 2 * i + c
-        first_row = pl.multiple_of(chunk * ROWS, ROWS)
-        pos = first_row + iota((ROWS, 64), 0)
+    def embed_rows(g):
+        begin = [pl.multiple_of((4 * g + 2 * e + c) * ROWS, ROWS) for e in range(2)]
+        step = iota((2 * ROWS, 64), 0)
+        pos = begin[0] + step + jnp.where(step >= ROWS, ROWS, 0)
         source, first, count = plan_ref[0], plan_ref[1], plan_ref[2]
         start = plan_ref[3] * ROWS + plan_ref[4]
         inside = (pos >= start) & (pos < start + count)
@@ -271,42 +265,53 @@
         code = jnp.sum(code.astype(F32), axis=1, keepdims=True).astype(jnp.int32)
         row_of = code % 512
         shard_of = code // 512
-        onehot = jnp.where(iota((ROWS, ROWS), 1) == row_of, 1.0, 0.0).astype(BF)
+        onehot = jnp.where(iota((2 * ROWS, ROWS), 1) == row_of, 1.0, 0.0).astype(BF)
         spread = dot_nt(onehot, xg[...])
         cols = jnp.where(
-            iota((ROWS, SEQ * PATCH), 1) // PATCH == shard_of, spread, 0.0
+            iota((2 * ROWS, SEQ * PATCH), 1) // PATCH == shard_of, spread, 0.0
         ).astype(BF)
         half = (dot(cols, win8[...]) + bin_ref[...].reshape(1, D)) * 0.5
         hidden = (half + half * jnp.tanh(half)).astype(BF)
-        emb = (dot(hidden, wh[...]) + dot(cols, wskip8[...]) + ob_ref[...].reshape(1, D)).astype(BF)
-
-        emb_own[i] = emb
-
+        emb = dot(hidden, wh[...]) + dot(cols, wskip8[...]) + ob_ref[...].reshape(1, D)
+        emb = emb.astype(BF)
+        emb_own[2 * g] = emb[:ROWS]
+        emb_own[2 * g + 1] = emb[ROWS:]
+        return begin, emb
+
+    def project_rows(g, begin, emb):
         wide = emb.astype(F32)
         scale = lax.rsqrt(jnp.mean(wide * wide, axis=-1, keepdims=True) + EPS)
         normed = (wide * scale * gain_ref[...].reshape(1, D)).astype(BF)
         proj = dot(normed, wsel[...]).astype(BF)
 
-        seg_row = seg_ref[:, pl.ds(first_row, ROWS)]
-        marks = jnp.where(iota((LANES, ROWS), 0) - HD == seg_row, 1.0, 0.0)
-        marks = jnp.transpose(marks)
+        marks = []
+        for e in range(2):
+            seg_row = seg_ref[:, pl.ds(begin[e], ROWS)]
+            match = jnp.where(iota((LANES, ROWS), 0) - HD == seg_row, 1.0, 0.0)
+            marks.append(jnp.transpose(match))
+        marks = jnp.concatenate(marks, axis=0)
         away = jnp.where(seg_lane, (marks - 1.0) * MASKED, 0.0)
         ones = jnp.where(lane == HD, 1.0, 0.0)
-        parts = []
-        for h in range(2):
+        for h in (1, 0):
             q = proj[:, (3 * h) * LANES : (3 * h + 1) * LANES].astype(F32)
             k = proj[:, (3 * h + 1) * LANES : (3 * h + 2) * LANES].astype(F32)
             v = proj[:, (3 * h + 2) * LANES : (3 * h + 3) * LANES].astype(F32)
             q = q * lax.rsqrt(jnp.sum(q * q, axis=-1, keepdims=True) * (1.0 / HD) + EPS)
             k = k * lax.rsqrt(jnp.sum(k * k, axis=-1, keepdims=True) * (1.0 / HD) + EPS)
-            parts.append([(q + away).astype(BF), (k + marks).astype(BF), (v + ones).astype(BF)])
-        for j in range(3):
-            msend[i, :, j * LANES : (j + 1) * LANES] = parts[1][j]
-        m_copy(i, c).start()
-        for j in range(3):
-            qkv[pl.ds(first_row, ROWS), j * LANES : (j + 1) * LANES] = parts[0][j]
-
-    embed_chunk(0)
+            parts = [(q + away).astype(BF), (k + marks).astype(BF), (v + ones).astype(BF)]
+            for e in range(2):
+                for j in range(3):
+                    part = parts[j][e * ROWS : (e + 1) * ROWS]
+                    lanes = slice(j * LANES, (j + 1) * LANES)
+                    if h:
+                        msend[2 * g + e, :, lanes] = part
+                    else:
+                        qkv[pl.ds(begin[e], ROWS), lanes] = part
+            if h:
+                m_copy(2 * g, c).start()
+                m_copy(2 * g + 1, c).start()
+
+    begin, emb = embed_rows(0)
     for k in range(1, ZN):
         w1_copy(k, (z - k + ZN) % ZN).wait_recv()
     for m in range(5):
@@ -322,7 +327,7 @@
     wx[xx] = block.astype(BF)
     for k in range(1, XN):
         w2_copy(k, None).start()
-    embed_chunk(1)
+    project_rows(0, begin, emb)
     for k in range(1, XN):
         w2_copy(k, (xx - k + XN) % XN).wait_recv()
     block = jnp.concatenate([wx[j, 0:GROUP, :].astype(F32) for j in range(XN)], axis=0)
@@ -330,11 +335,7 @@
     for k in range(1, YN):
         w3_copy(k, s).start()
     w4_copy(0, c).start()
-    embed_chunk(2)
-    embed_chunk(3)
-    for i in range(4):
-        m_copy(i, 1 - c).wait_recv()
-
+    project_rows(1, *embed_rows(1))
     factor = hs_ref[s] * (LOG2E / math.sqrt(HD))
     causal = iota((ROWS, ROWS), 0) >= iota((ROWS, ROWS), 1)
 
@@ -342,7 +343,12 @@
         rows = ret.at[pl.ds(pl.multiple_of(source * HD, 16), HD), :]
         return rcopy(att_send.at[block], rows, a_s.at[k], a_r.at[k], dp, (s + k) % SEQ)
 
-    for b in reversed(range(SEQ)):
+    for i in range(2):
+        m_copy(i, 1 - c).wait_recv()
+    for b in (3, 2, 7, 0, 5, 1, 6, 4):
+        if b == 7:
+            for i in range(2, 4):
+                m_copy(i, 1 - c).wait_recv()
         q = qkv[b * ROWS : (b + 1) * ROWS, 0:LANES]
         total = jnp.zeros((ROWS, LANES), F32)
         edges = list(range(0, b * ROWS, 2 * ROWS)) + [b * ROWS]
@@ -365,7 +371,7 @@
         def _():
             a_copy(b, s, (b - s + SEQ) % SEQ).start()
 
-        if b == 3:
+        if b == 5:
             for k in range(1, YN):
                 w3_copy(k, ((y - k + YN) % YN) * 2 + c).wait_recv()
                 w4_copy(k, c).start()
@@ -413,9 +419,12 @@
         to = (y + k) % YN
         return rcopy(ya.at[to], ya_land.at[k], ya_s.at[k], ya_r.at[k], dp, to * 2 + c)
 
-    def xb_copy(k):
+    def xb_copy(k, row):
         to = (xx + k) % XN
-        return rcopy(xb.at[to], xb_land.at[k], xb_s.at[k], xb_r.at[k], dpi(z, to), s)
+        slot = k * YN + row
+        return rcopy(
+            xb.at[to, row], xb_land.at[k, row], xb_s.at[slot], xb_r.at[slot], dpi(z, to), s
+        )
 
     pad = jnp.zeros((8, HW - ROWS), F32)
     for k in order:
@@ -429,8 +438,8 @@
         for j in range(XN):
             part = piece[j * GROUP : (j + 1) * GROUP, ROWS:]
             xb[j, to] = jnp.concatenate([part, pad], axis=0).astype(BF)
-    for k in (2, 1, 3):
-        xb_copy(k).start()
+        for j in (2, 1, 3):
+            xb_copy(j, to).start()
 
     rows = jnp.transpose(attended)
     for j in range(5):
@@ -463,7 +472,8 @@
         ax_copy(k).start()
 
     for k in range(1, XN):
-        xb_copy(k).wait_recv()
+        for j in range(YN):
+            xb_copy(k, j).wait_recv()
     pad = jnp.zeros((8, HW - ROWS), F32)
     for j in range(YN):
         begin = pl.multiple_of((j * XN + xx) * GROUP, 8)
@@ -525,13 +535,25 @@
         w2_copy(k, None).wait_send()
         w3_copy(k, s).wait_send()
         ya_copy(k).wait_send()
-        xb_copy(k).wait_send()
+        for j in range(YN):
+            xb_copy(k, j).wait_send()
         ax_copy(k).wait_send()
         by_copy(k).wait_send()
     for k in range(YN):
         w4_copy(k, c).wait_send()
         m_copy(k, c).wait_send()
         p_copy(k).wait_send()
+
+
+def hand_over(lo_in, og_in, lo_out, og_out, sem):
+    copies = [pltpu.make_async_copy(og_in, og_out, sem.at[0])]
+    for j in range(4):
+        rows = pl.ds(j * 96, 96)
+        copies.append(pltpu.make_async_copy(lo_in.at[rows, :], lo_out.at[rows, :], sem.at[j + 1]))
+    for copy in copies:
+        copy.start()
+    for copy in copies:
+        copy.wait()
 
 
 def per_device(
@@ -553,7 +575,6 @@
     hbm = pl.BlockSpec(memory_space=pltpu.HBM)
     dma = pltpu.SemaphoreType.DMA
     scratch = [
-        pltpu.VMEM((PATCH, ROWS), BF),
         pltpu.VMEM((1, WIN), jnp.int32),
         pltpu.VMEM((5, 1, 64), jnp.int32),
         pltpu.VMEM((PATCH, D), BF),
@@ -617,8 +638,8 @@
         dma((4,)),
         dma((4,)),
         dma((4,)),
-        dma((4,)),
-        dma((4,)),
+        dma((16,)),
+        dma((16,)),
         dma((4,)),
         dma((4,)),
         dma((4,)),
@@ -654,6 +675,17 @@
         jnp.transpose(out_weight),
         cotangent,
     )
+    layer_out, grad = pl.pallas_call(
+        hand_over,
+        out_shape=(
+            jax.ShapeDtypeStruct((ROWS, D), BF),
+            jax.ShapeDtypeStruct((COLS, HW), F32),
+        ),
+        in_specs=[hbm, hbm],
+        out_specs=(hbm, hbm),
+        scratch_shapes=[dma((5,))],
+        name="hand_over",
+    )(layer_out, grad)
     return layer_out, jnp.transpose(grad)
 
 

time: 72.9 us -> 99.3 us (1.36); the launches traced: 71.8 us -> 99.2 us
  Pallas kernels: 67.6 us -> 98.4 us
  local copies, waits for them, and re-layouts: 3.54 us -> 0 us
    pallas_call x0 -> x1, Pallas kernels: none -> 31.5 us  [per_device(): pl.pallas_call(hand_over, out_shape=(jax.ShapeDtypeStruct((ROWS, D), BF),...]
    unnamed x2 -> x0, local copies, waits for them, and re-layouts: 3.54 us -> none
where the time goes in v3:
time: 99.3 us; the launch traced here: 99.2 us
  Pallas kernels  98.4 us (99%)
    pallas_call x1, Pallas kernels, per_device(): pl.pallas_call(whole_layer, out_shape=(jax.ShapeDtypeStruct((ROWS, D), BF...  66.9 us
    pallas_call x1, Pallas kernels, per_device(): pl.pallas_call(hand_over, out_shape=(jax.ShapeDtypeStruct((ROWS, D), BF),...  31.5 us

profile of v3, /device:TPU:1, one launch (start us, length us, event | category | flops | bytes accessed | tf_op | source)
XLA Modules:
  0.0 99.2 jit_solution(7058712360347551287)
XLA Ops:
  0.6 66.9 %whole_layer.1 = (bf16[384,1280]{1,0:T(8,128)(2,1)}, f32[5,640]{1,0:T(8,128)}) custom-call(bf16[32,384]{1,0:T(8,128)(2,1)} %x_hbm.1, s32[1,3072]{1,0:T(1,128)} %seg_hbm.1, s32[5,1,64]{2,1,0:T(1,128)} %bitcast.6, bf16[32,1280]{1,0:T(8,128)(2,1)} %win_hbm.1, f32[1280]{0:T(1024)} %bin_hbm.1, bf16[32,1280]{1,0:T(8,128)(2,1)} %wskip_hbm.1, ...), custom_call_target="tpu_custom_call" | custom-call | tf_op jit(solution)/shard_map/whole_layer/pallas_call | solution.py:650
  67.5 31.5 %hand_over.1 = (bf16[384,1280]{1,0:T(8,128)(2,1)}, f32[5,640]{1,0:T(8,128)}) custom-call(bf16[384,1280]{1,0:T(8,128)(2,1)} %get-tuple-element.6.lo_in, f32[5,640]{1,0:T(8,128)} %get-tuple-element.7.og_in), custom_call_target="tpu_custom_call" | custom-call | tf_op jit(solution)/shard_map/hand_over/pallas_call | solution.py:678

commit v4 on v3

--- a/solution.py
+++ b/solution.py
@@ -545,14 +545,26 @@
         p_copy(k).wait_send()
 
 
-def hand_over(lo_in, og_in, lo_out, og_out, sem):
-    copies = [pltpu.make_async_copy(og_in, og_out, sem.at[0])]
-    for j in range(4):
-        rows = pl.ds(j * 96, 96)
-        copies.append(pltpu.make_async_copy(lo_in.at[rows, :], lo_out.at[rows, :], sem.at[j + 1]))
-    for copy in copies:
+def hand_over(lo_in, og_in, lo_out, og_out, lo_vmem, og_vmem, sem_in, sem_out):
+    def parts(lo, og):
+        rows = [pl.ds(k * 128, 128) for k in range(3)]
+        return [lo.at[r, :] for r in rows] + [og]
+
+    held = parts(lo_vmem, og_vmem)
+    into = [
+        pltpu.make_async_copy(a, b, sem_in.at[k])
+        for k, (a, b) in enumerate(zip(parts(lo_in, og_in), held))
+    ]
+    back = [
+        pltpu.make_async_copy(a, b, sem_out.at[k])
+        for k, (a, b) in enumerate(zip(held, parts(lo_out, og_out)))
+    ]
+    for copy in into:
         copy.start()
-    for copy in copies:
+    for a, b in zip(into, back):
+        a.wait()
+        b.start()
+    for copy in back:
         copy.wait()
 
 
@@ -683,7 +695,12 @@
         ),
         in_specs=[hbm, hbm],
         out_specs=(hbm, hbm),
-        scratch_shapes=[dma((5,))],
+        scratch_shapes=[
+            pltpu.VMEM((ROWS, D), BF),
+            pltpu.VMEM((COLS, HW), F32),
+            dma((4,)),
+            dma((4,)),
+        ],
         name="hand_over",
     )(layer_out, grad)
     return layer_out, jnp.transpose(grad)

time: 99.3 us -> 69.8 us (0.70)
  Pallas kernels: 98.4 us -> 68.8 us
    pallas_call x1, Pallas kernels: 31.5 us -> 1.98 us  [per_device(): pl.pallas_call(hand_over, out_shape=(jax.ShapeDtypeStruct((ROWS, D), BF),...]
where the time goes in v4:
time: 69.8 us; the launch traced here: 69.7 us
  Pallas kernels  68.8 us (99%)
  between operations  0.82 us (1%)
    pallas_call x1, Pallas kernels, per_device(): pl.pallas_call(whole_layer, out_shape=(jax.ShapeDtypeStruct((ROWS, D), BF...  66.9 us
    pallas_call x1, Pallas kernels, per_device(): pl.pallas_call(hand_over, out_shape=(jax.ShapeDtypeStruct((ROWS, D), BF),...  1.98 us

profile of v4, /device:TPU:1, one launch (start us, length us, event | category | flops | bytes accessed | tf_op | source)
XLA Modules:
  0.0 69.7 jit_solution(17363813792362655507)
XLA Ops:
  0.6 66.9 %whole_layer.1 = (bf16[384,1280]{1,0:T(8,128)(2,1)}, f32[5,640]{1,0:T(8,128)}) custom-call(bf16[32,384]{1,0:T(8,128)(2,1)} %x_hbm.1, s32[1,3072]{1,0:T(1,128)} %seg_hbm.1, s32[5,1,64]{2,1,0:T(1,128)} %bitcast.6, bf16[32,1280]{1,0:T(8,128)(2,1)} %win_hbm.1, f32[1280]{0:T(1024)} %bin_hbm.1, bf16[32,1280]{1,0:T(8,128)(2,1)} %wskip_hbm.1, ...), custom_call_target="tpu_custom_call" | custom-call | tf_op jit(solution)/shard_map/whole_layer/pallas_call | solution.py:662
  67.5 2.0 %hand_over.1 = (bf16[384,1280]{1,0:T(8,128)(2,1)}, f32[5,640]{1,0:T(8,128)}) custom-call(bf16[384,1280]{1,0:T(8,128)(2,1)} %get-tuple-element.6.lo_in, f32[5,640]{1,0:T(8,128)} %get-tuple-element.7.og_in), custom_call_target="tpu_custom_call" | custom-call | tf_op jit(solution)/shard_map/hand_over/pallas_call | solution.py:690

commit v5 on v4

--- a/solution.py
+++ b/solution.py
@@ -86,8 +86,7 @@
     att_send,
     ret,
     p_own,
-    p_send,
-    p_land,
+    cot_m,
     ya,
     ya_land,
     xb,
@@ -117,6 +116,8 @@
     a_r,
     p_s,
     p_r,
+    c_s,
+    c_r,
     ya_s,
     ya_r,
     xb_s,
@@ -339,9 +340,28 @@
     factor = hs_ref[s] * (LOG2E / math.sqrt(HD))
     causal = iota((ROWS, ROWS), 0) >= iota((ROWS, ROWS), 1)
 
-    def a_copy(block, source, k):
-        rows = ret.at[pl.ds(pl.multiple_of(source * HD, 16), HD), :]
+    def head_rows(core, head):
+        return ret.at[core, pl.ds(pl.multiple_of(head * HD, 16), HD), :]
+
+    def a_copy(block, source, k, core):
+        rows = head_rows(core, source)
         return rcopy(att_send.at[block], rows, a_s.at[k], a_r.at[k], dp, (s + k) % SEQ)
+
+    def c_copy():
+        return rcopy(cot_t.at[1 - c], cot_m, c_s.at[0], c_r.at[0], dp, mate)
+
+    def cotangent_columns():
+        loads[12].wait()
+        for m in range(3):
+            cot_f[m] = jnp.transpose(cot[m * LANES : (m + 1) * LANES, :].astype(F32))
+        for core in range(2):
+            for j in range(YN):
+                base = [x2 * GROUP + (2 * j + core) * COLS + n for x2 in range(XN) for n in range(COLS)]
+                for m in range(3):
+                    rows = [cot_f[m, pl.ds(first, ZN, stride=160), :] for first in base]
+                    rows = jnp.concatenate(rows, axis=0).astype(BF)
+                    cot_t[core, j * 160 : (j + 1) * 160, m * LANES : (m + 1) * LANES] = rows
+        c_copy().start()
 
     for i in range(2):
         m_copy(i, 1 - c).wait_recv()
@@ -365,27 +385,19 @@
 
         @pl.when(s == b)
         def _():
-            ret[pl.ds(pl.multiple_of(s * HD, 16), HD), :] = out
+            ret[c, pl.ds(pl.multiple_of(s * HD, 16), HD), :] = out
 
         @pl.when(s != b)
         def _():
-            a_copy(b, s, (b - s + SEQ) % SEQ).start()
-
+            a_copy(b, s, (b - s + SEQ) % SEQ, b % 2).start()
+
+        if b == 0:
+            cotangent_columns()
         if b == 5:
             for k in range(1, YN):
                 w3_copy(k, ((y - k + YN) % YN) * 2 + c).wait_recv()
                 w4_copy(k, c).start()
 
-    loads[12].wait()
-    for m in range(3):
-        cot_f[m] = jnp.transpose(cot[m * LANES : (m + 1) * LANES, :].astype(F32))
-    for core in range(2):
-        for j in range(YN):
-            base = [x2 * GROUP + (2 * j + core) * COLS + n for x2 in range(XN) for n in range(COLS)]
-            for m in range(3):
-                rows = [cot_f[m, pl.ds(first, ZN, stride=160), :] for first in base]
-                rows = jnp.concatenate(rows, axis=0).astype(BF)
-                cot_t[core, j * 160 : (j + 1) * 160, m * LANES : (m + 1) * LANES] = rows
     for k in range(YN):
         w4_copy(k, 1 - c).wait_recv()
     for t in range(SEQ):
@@ -397,23 +409,28 @@
                 for m in range(5):
                     wt_f[m, rows, :] = block[first : first + ZN, m * LANES : (m + 1) * LANES]
 
+    def pass_on(head, core):
+        return rcopy(
+            head_rows(core, head), head_rows(core, head), p_s.at[head], p_r.at[head], dp, mate
+        )
+
+    pass_on(s, c).start()
     for k in range(1, SEQ):
-        a_copy(0, (s - k + SEQ) % SEQ, k).wait_recv()
-
-    attended = ret[...]
+        head = (s - k + SEQ) % SEQ
+        a_copy(0, head, k, c).wait_recv()
+        pass_on(head, c).start()
+
+    attended = ret[c]
     order = [2, 1, 3, 0]
-
-    def p_copy(k):
-        piece = (y + k) % YN
-        return rcopy(p_send.at[piece], p_land.at[piece], p_s.at[k], p_r.at[k], dp, mate)
 
     def owner_rows(k):
         return pl.ds(pl.multiple_of(((y + k) % YN) * 160, 32), 160)
 
-    for k in order:
-        p_send[(y + k) % YN] = dot_nt(cot_t[1 - c, owner_rows(k), :], attended).astype(BF)
-        p_copy(k).start()
     p_own[...] = dot_nt(cot_t[c], attended)
+    c_copy().wait_recv()
+    for head in range(SEQ):
+        pass_on(head, 1 - c).wait_recv()
+    other = ret[1 - c]
 
     def ya_copy(k):
         to = (y + k) % YN
@@ -429,8 +446,7 @@
     pad = jnp.zeros((8, HW - ROWS), F32)
     for k in order:
         to = (y + k) % YN
-        p_copy(k).wait_recv()
-        piece = p_own[owner_rows(k), :] + p_land[to].astype(F32)
+        piece = p_own[owner_rows(k), :] + dot_nt(cot_m[owner_rows(k), :], other)
         p_own[owner_rows(k), :] = piece
         if k:
             ya[to] = piece[:, 0:ROWS].astype(BF)
@@ -527,7 +543,7 @@
 
     for k in range(1, SEQ):
         x_copy(k, s).wait_send()
-        a_copy(0, s, k).wait_send()
+        a_copy(0, s, k, (s + k) % 2).wait_send()
     for k in range(1, ZN):
         w1_copy(k, z).wait_send()
         f_copy(k).wait_send()
@@ -542,7 +558,9 @@
     for k in range(YN):
         w4_copy(k, c).wait_send()
         m_copy(k, c).wait_send()
-        p_copy(k).wait_send()
+    for head in range(SEQ):
+        pass_on(head, c).wait_send()
+    c_copy().wait_send()
 
 
 def hand_over(lo_in, og_in, lo_out, og_out, lo_vmem, og_vmem, sem_in, sem_out):
@@ -615,10 +633,9 @@
         pltpu.VMEM((5, D, LANES), F32),
         pltpu.VMEM((5, 64, LANES), F32),
         pltpu.VMEM((SEQ, HD, ROWS), BF),
+        pltpu.VMEM((2, HW, ROWS), BF),
+        pltpu.VMEM((HW, HW), F32),
         pltpu.VMEM((HW, ROWS), BF),
-        pltpu.VMEM((HW, HW), F32),
-        pltpu.VMEM((YN, 160, HW), BF),
-        pltpu.VMEM((YN, 160, HW), BF),
         pltpu.VMEM((YN, 160, ROWS), BF),
         pltpu.VMEM((YN, 160, ROWS), BF),
         pltpu.VMEM((XN, YN, 48, HW - ROWS), BF),
@@ -646,8 +663,10 @@
         dma((4,)),
         dma((8,)),
         dma((8,)),
-        dma((4,)),
-        dma((4,)),
+        dma((8,)),
+        dma((8,)),
+        dma((1,)),
+        dma((1,)),
         dma((4,)),
         dma((4,)),
         dma((16,)),

time: 69.8 us -> 70.1 us (level)
  no operation moved by 1% of the time
where the time goes in v5:
time: 70.1 us; the launch traced here: 70 us
  Pallas kernels  69.2 us (99%)
  between operations  0.82 us (1%)
    pallas_call x1, Pallas kernels, per_device(): pl.pallas_call(whole_layer, out_shape=(jax.ShapeDtypeStruct((ROWS, D), BF...  67.2 us
    pallas_call x1, Pallas kernels, per_device(): pl.pallas_call(hand_over, out_shape=(jax.ShapeDtypeStruct((ROWS, D), BF),...  1.98 us

profile of v5, /device:TPU:1, one launch (start us, length us, event | category | flops | bytes accessed | tf_op | source)
XLA Modules:
  0.0 70.0 jit_solution(13877408841374794396)
XLA Ops:
  0.6 67.2 %whole_layer.1 = (bf16[384,1280]{1,0:T(8,128)(2,1)}, f32[5,640]{1,0:T(8,128)}) custom-call(bf16[32,384]{1,0:T(8,128)(2,1)} %x_hbm.1, s32[1,3072]{1,0:T(1,128)} %seg_hbm.1, s32[5,1,64]{2,1,0:T(1,128)} %bitcast.6, bf16[32,1280]{1,0:T(8,128)(2,1)} %win_hbm.1, f32[1280]{0:T(1024)} %bin_hbm.1, bf16[32,1280]{1,0:T(8,128)(2,1)} %wskip_hbm.1, ...), custom_call_target="tpu_custom_call" | custom-call | tf_op jit(solution)/shard_map/whole_layer/pallas_call | solution.py:681
  67.8 2.0 %hand_over.1 = (bf16[384,1280]{1,0:T(8,128)(2,1)}, f32[5,640]{1,0:T(8,128)}) custom-call(bf16[384,1280]{1,0:T(8,128)(2,1)} %get-tuple-element.6.lo_in, f32[5,640]{1,0:T(8,128)} %get-tuple-element.7.og_in), custom_call_target="tpu_custom_call" | custom-call | tf_op jit(solution)/shard_map/hand_over/pallas_call | solution.py:709

commit v6 on v5

--- a/solution.py
+++ b/solution.py
@@ -72,7 +72,6 @@
     cot_t,
     xg,
     win8,
-    wskip8,
     wsel,
     qkv,
     msend,
@@ -176,7 +175,7 @@
                 (ob_hbm, ob_ref),
                 (gain_hbm, gain_ref),
                 (hs_hbm, hs_ref),
-                (wh_hbm, wh),
+                (wh_hbm, wh.at[pl.ds(0, D), :]),
                 (cot_hbm, cot),
             ]
         )
@@ -210,7 +209,7 @@
         ld.wait()
     for k in range(SEQ):
         win8[k * PATCH : (k + 1) * PATCH, :] = win_ref[...]
-        wskip8[k * PATCH : (k + 1) * PATCH, :] = wskip_ref[...]
+        wh[D + k * PATCH : D + (k + 1) * PATCH, :] = wskip_ref[...]
 
     loads[4].wait()
     feature = iota((2 * LANES, 2 * LANES), 0) + y * LANES
@@ -273,8 +272,8 @@
         ).astype(BF)
         half = (dot(cols, win8[...]) + bin_ref[...].reshape(1, D)) * 0.5
         hidden = (half + half * jnp.tanh(half)).astype(BF)
-        emb = dot(hidden, wh[...]) + dot(cols, wskip8[...]) + ob_ref[...].reshape(1, D)
-        emb = emb.astype(BF)
+        both = jnp.concatenate([hidden, cols], axis=1)
+        emb = (dot(both, wh[...]) + ob_ref[...].reshape(1, D)).astype(BF)
         emb_own[2 * g] = emb[:ROWS]
         emb_own[2 * g + 1] = emb[ROWS:]
         return begin, emb
@@ -614,13 +613,12 @@
         pltpu.VMEM((D,), F32),
         pltpu.SMEM((SEQ,), F32),
         pltpu.VMEM((COLS, HW), BF),
-        pltpu.VMEM((D, D), BF),
+        pltpu.VMEM((D + SEQ * PATCH, D), BF),
         pltpu.VMEM((3, D, 2 * LANES), BF),
         pltpu.VMEM((ROWS, D), BF),
         pltpu.VMEM((3, D, LANES), F32),
         pltpu.VMEM((2, HW, ROWS), BF),
         pltpu.VMEM((SEQ * PATCH, ROWS), BF),
-        pltpu.VMEM((SEQ * PATCH, D), BF),
         pltpu.VMEM((SEQ * PATCH, D), BF),
         pltpu.VMEM((D, 6 * LANES), BF),
         pltpu.VMEM((WIN, 3 * LANES), BF),

time: 70.1 us -> 70.1 us (level)
  no operation moved by 1% of the time
where the time goes in v6:
time: 70.1 us; the launch traced here: 70 us
  Pallas kernels  69.2 us (99%)
  between operations  0.82 us (1%)
    pallas_call x1, Pallas kernels, per_device(): pl.pallas_call(whole_layer, out_shape=(jax.ShapeDtypeStruct((ROWS, D), BF...  67.2 us
    pallas_call x1, Pallas kernels, per_device(): pl.pallas_call(hand_over, out_shape=(jax.ShapeDtypeStruct((ROWS, D), BF),...  1.98 us

profile of v6, /device:TPU:1, one launch (start us, length us, event | category | flops | bytes accessed | tf_op | source)
XLA Modules:
  0.0 70.0 jit_solution(940821985460411342)
XLA Ops:
  0.6 67.2 %whole_layer.1 = (bf16[384,1280]{1,0:T(8,128)(2,1)}, f32[5,640]{1,0:T(8,128)}) custom-call(bf16[32,384]{1,0:T(8,128)(2,1)} %x_hbm.1, s32[1,3072]{1,0:T(1,128)} %seg_hbm.1, s32[5,1,64]{2,1,0:T(1,128)} %bitcast.6, bf16[32,1280]{1,0:T(8,128)(2,1)} %win_hbm.1, f32[1280]{0:T(1024)} %bin_hbm.1, bf16[32,1280]{1,0:T(8,128)(2,1)} %wskip_hbm.1, ...), custom_call_target="tpu_custom_call" | custom-call | tf_op jit(solution)/shard_map/whole_layer/pallas_call | solution.py:679
  67.8 2.0 %hand_over.1 = (bf16[384,1280]{1,0:T(8,128)(2,1)}, f32[5,640]{1,0:T(8,128)}) custom-call(bf16[384,1280]{1,0:T(8,128)(2,1)} %get-tuple-element.6.lo_in, f32[5,640]{1,0:T(8,128)} %get-tuple-element.7.og_in), custom_call_target="tpu_custom_call" | custom-call | tf_op jit(solution)/shard_map/hand_over/pallas_call | solution.py:707
